TPU v7x, 256 devices: a whole 4x4x8 slice. The times are simulated.
256 devices in a mesh: dp: 32 (over z, y), tensor: 8 (over x, core).
Axes of the slice: x: 4, y: 4, z: 8, core: 2. Of those that a mesh axis runs over, the one named last changes fastest.
Arguments:
- inputs: bfloat16 [2, 4096, 4096], P(None, 'dp', 'tensor'), may hold values from -6 to 6
- out_grads: bfloat16 [2, 4096, 4096], P(None, 'dp', 'tensor'), may hold values from -6 to 6
- momentum: bfloat16 [32, 4096, 4096], P('dp', None, 'tensor'), may hold values from -6 to 6
- band: int32 [64, 64, 2, 8], P(None, 'tensor'), may hold values from 0 to 15, as said below
Outputs:
- new_momentum: bfloat16 [32, 4096, 4096], P('dp', None, 'tensor')
- update: float32 [4096, 4096], P('dp', 'tensor')
Inputs may be any that keep to these rules, and one draw needn't show every extreme that they name: Each band[r, c, s, :] holds 8 different frequencies of 0 to 15 in rising order.
All inputs are finite; a program needn't handle non-finite values.
Results may differ from a plain program's by a relative error of at most 0.001.
Values may be sent and summed in bfloat16 or wider, within the bound.
A program may use at most 128 MiB of HBM per device.

v0:
```python
import math

import jax
import jax.numpy as jnp
from jax import lax
from jax.sharding import PartitionSpec as P

SPAN = 64
LOW = 16
STEPS = 2


def dct_basis(order):
    freq = jnp.arange(order, dtype=jnp.float32)[:, None]
    place = jnp.arange(order, dtype=jnp.float32)[None, :]
    table = jnp.sqrt(2.0 / order) * jnp.cos(math.pi * (2.0 * place + 1.0) * freq / (2.0 * order))
    first = jnp.where(jnp.arange(order)[:, None] == 0, 1.0 / math.sqrt(2.0), 1.0)
    return table * first


def decode_low(grid, low_rows, col_table, side):
    lowest = low_rows.shape[0]
    wide = jnp.dot(grid, col_table.T, precision=lax.Precision.HIGHEST)
    wide = wide.reshape(grid.shape[0] // lowest, lowest, col_table.shape[0])
    full = jnp.einsum("ki,rkj->rij", low_rows, wide, precision=lax.Precision.HIGHEST)
    return full.reshape(full.shape[0] * side, col_table.shape[0])


def shards(inputs, out_grads, momentum, band):
    side = SPAN
    lowest = LOW
    basis = dct_basis(side)
    low_rows = basis[:lowest]
    span_rows = band.shape[0]
    span_cols = band.shape[1]
    out_local = momentum.shape[2]
    col_table = jnp.kron(jnp.eye(span_cols, dtype=jnp.float32), low_rows.T)
    member = jnp.sum(
        (band[..., None] == jnp.arange(lowest, dtype=jnp.int32)).astype(jnp.float32), axis=3
    )
    keep_mask = jnp.einsum("rck,rcl->rkcl", member[:, :, 0], member[:, :, 1]).reshape(
        span_rows * lowest, span_cols * lowest
    )
    factor = 1.0 / math.sqrt(inputs.shape[1])
    groups = lax.axis_size("dp")
    own = span_rows // groups
    begin = lax.axis_index("dp") * own * lowest
    state = momentum[0].astype(jnp.float32)
    update = jnp.zeros((own * side, out_local), jnp.float32)
    for step in range(STEPS):
        right = out_grads[step]
        grad = (
            lax.dot_general(
                lax.all_gather(inputs[step], "tensor", axis=1, tiled=True),
                right,
                (((0,), (0,)), ((), ())),
                preferred_element_type=jnp.float32,
            )
            * factor
        )
        state = 0.9 * state + grad
        tall = jnp.einsum(
            "ki,rij->rkj",
            low_rows,
            state.reshape(span_rows, side, out_local),
            precision=lax.Precision.HIGHEST,
        )
        grid = (
            jnp.dot(
                tall.reshape(span_rows * lowest, out_local),
                col_table,
                precision=lax.Precision.HIGHEST,
            )
            * keep_mask
        )
        state = state - decode_low(grid, low_rows, col_table, side)
        summed = lax.psum(grid, "dp")
        mine = lax.dynamic_slice_in_dim(summed, begin, own * lowest, 0)
        update = update + decode_low(mine, low_rows, col_table, side)
    new_momentum = state.astype(jnp.bfloat16)[None]
    return (new_momentum, update)


def solution(mesh):
    return jax.shard_map(
        shards,
        mesh=mesh,
        in_specs=(
            P(None, "dp", "tensor"),
            P(None, "dp", "tensor"),
            P("dp", None, "tensor"),
            P(None, "tensor", None, None),
        ),
        out_specs=(P("dp", None, "tensor"), P("dp", "tensor")),
        check_vma=False,
    )
```

profile of v0, /device:TPU:5, one launch (start us, length us, event | category | flops | bytes accessed | tf_op | source)
XLA Modules:
  0.0 244.9 jit_solution(12087409868376257689)
XLA Ops:
  7.2 0.0 copy-start.4
  7.2 0.0 all-gather.5.cloned.1.call-start
  7.2 1.7 fusion.71
  8.9 0.0 all-gather.5.cloned.1.call-update
  9.0 0.0 all-gather.7.cloned.1.call-start
  9.0 0.7 all-gather.7.cloned.1.call-update
  9.7 0.1 fusion.21
  9.8 0.1 broadcast_multiply_fusion
  9.9 0.1 mul.237
  10.1 1.0 convert_reduce_fusion
  11.1 0.3 copy.12
  11.4 0.1 copy.11
  11.5 3.1 %multiply_bitcast_fusion = f32[64,16,8,16]{3,2,1,0:T(8,128)} fusion(f32[64,8,16]{1,2,0:T(8,128)S(1)} %copy.12, f32[64,8,16]{2,1,0:T(8,128)S(1)} %copy.11), kind=kLoop, calls=%fused_computation.6 | loop fusion | flops 131072 | bytes 589824 | tf_op jit(solution)/shard_map/rck,rcl->rkcl/transpose | solution.py:41
  14.6 3.2 %reshape.101 = f32[1024,128]{1,0:T(8,128)S(1)} reshape(f32[64,16,8,16]{3,2,1,0:T(8,128)} %multiply_bitcast_fusion) | data formatting | bytes 1048576 | tf_op jit(solution)/shard_map/reshape | solution.py:41
  17.9 19.8 %all-gather.5.cloned.1.call-done = bf16[1,128,4096]{2,1,0:T(8,128)(2,1)} async-done(((bf16[1,128,512]{2,1,0:T(8,128)(2,1)}), bf16[1,128,4096]{2,1,0:T(8,128)(2,1)}) %all-gather.5.cloned.1.call-update) | async-done | bytes 1048592 | tf_op jit(solution)/shard_map/all_gather | solution.py:54
  37.7 0.0 copy-done.4
  37.7 4.0 %bitcast_add_fusion = f32[4096,512]{1,0:T(8,128)S(1)} fusion(bf16[1,4096,512]{2,1,0:T(8,128)(2,1)} %param.6, bf16[1,128,4096]{2,1,0:T(8,128)(2,1)} %all-gather.5.cloned.1.call-done, bf16[2,128,512]{2,1,0:T(8,128)(2,1)S(1)} %copy-done.4), kind=kOutput, calls=%fused_computation.5 | convolution fusion | flops 545259520 | bytes 13762560 | tf_op jit(solution)/shard_map/dot_general | solution.py:53
  41.7 0.0 copy-start
  41.7 4.6 %fusion.31 = f32[64,512,16]{1,2,0:T(8,128)S(1)} fusion(f32[64,64,512]{2,1,0:T(8,128)S(1)} %bitcast.93, f32[16]{0:T(128)S(1)} %bitcast.104, f32[64]{0:T(128)S(1)} %add_multiply_fusion.1), kind=kOutput, calls=%fused_computation.39 | convolution fusion | flops 402658304 | bytes 10486080 | tf_op jit(solution)/shard_map/ki,rij->rkj/dot_general | solution.py:62
  46.3 1.8 convolution_multiply_fusion.1
  48.1 0.0 copy-start.2
  48.1 1.8 fusion.11
  49.9 0.0 copy-done
  49.9 9.3 %fusion.29 = f32[64,512,64]{1,2,0:T(8,128)} fusion(f32[64,16,512]{2,1,0:T(8,128)S(1)} %fusion.11, f32[16]{0:T(128)S(1)} %bitcast.105, f32[64]{0:T(128)S(1)} %add_multiply_fusion.1), kind=kOutput, calls=%fused_computation.38 | convolution fusion | flops 402658304 | bytes 10486080 | tf_op jit(solution)/shard_map/ki,rkj->rij/dot_general | solution.py:25
  59.3 6.7 %all-gather.7.cloned.1.call-done = bf16[1,128,4096]{2,1,0:T(8,128)(2,1)} async-done(((bf16[1,128,512]{2,1,0:T(8,128)(2,1)}), bf16[1,128,4096]{2,1,0:T(8,128)(2,1)}) %all-gather.7.cloned.1.call-update) | async-done | bytes 1048592 | tf_op jit(solution)/shard_map/all_gather | solution.py:54
  66.0 7.8 %fusion.2 = f32[4096,512]{1,0:T(8,128)S(1)} fusion(f32[4096,512]{1,0:T(8,128)} %copy-done, f32[64,512,64]{1,2,0:T(8,128)} %fusion.29, bf16[1,128,4096]{2,1,0:T(8,128)(2,1)} %all-gather.7.cloned.1.call-done, bf16[2,128,512]{2,1,0:T(8,128)(2,1)S(1)} %copy-done.4), kind=kOutput, calls=%fused_computation.4 | convolution fusion | flops 545259520 | bytes 26345472 | tf_op jit(solution)/shard_map/dot_general | solution.py:53
  73.8 0.0 copy-done.2
  73.8 0.0 copy-start.1
  73.8 3.2 %copy-done.1 = f32[4096,512]{1,0:T(8,128)} copy-done((f32[4096,512]{1,0:T(8,128)}, f32[4096,512]{1,0:T(8,128)S(1)}, u32[]{:S(2)}) %copy-start.1) | copy-done | bytes 8388632
  77.0 4.6 %fusion.27 = f32[64,512,16]{1,2,0:T(8,128)S(1)} fusion(f32[64,64,512]{2,1,0:T(8,128)S(1)} %bitcast.94, f32[16]{0:T(128)S(1)} %bitcast.106, f32[64]{0:T(128)S(1)} %add_multiply_fusion.1), kind=kOutput, calls=%fused_computation.37 | convolution fusion | flops 402658304 | bytes 10486080 | tf_op jit(solution)/shard_map/ki,rij->rkj/dot_general | solution.py:62
  81.6 1.8 convolution_multiply_fusion
  83.4 0.0 copy-start.3
  83.4 1.8 fusion.9
  85.2 0.0 all-reduce.3.cloned.1.call-start
  85.3 0.0 copy-done.3
  85.3 0.7 all-reduce.3.cloned.1.call-update
  85.9 9.4 %fusion.25 = f32[64,512,64]{1,2,0:T(8,128)} fusion(f32[64,16,512]{2,1,0:T(8,128)S(1)} %fusion.9, f32[16]{0:T(128)S(1)} %bitcast.107, f32[64]{0:T(128)S(1)} %add_multiply_fusion.1), kind=kOutput, calls=%fused_computation.36 | convolution fusion | flops 402658304 | bytes 10486080 | tf_op jit(solution)/shard_map/ki,rkj->rij/dot_general | solution.py:25
  95.3 9.5 %fusion = bf16[4096,512]{1,0:T(8,128)(2,1)} fusion(f32[4096,512]{1,0:T(8,128)} %copy-done.1, f32[64,512,64]{1,2,0:T(8,128)} %fusion.25), kind=kLoop, calls=%fused_computation.1 | loop fusion | flops 4194304 | bytes 20971520 | tf_op jit(solution)/shard_map/convert_element_type | solution.py:80
  104.8 130.7 %all-reduce.3.cloned.1.call-done = (f32[1024,128]{1,0:T(8,128)}, f32[1024,128]{1,0:T(8,128)}) async-done(((f32[1024,128]{1,0:T(8,128)}, f32[1024,128]{1,0:T(8,128)}), (f32[1024,128]{1,0:T(8,128)}, f32[1024,128]{1,0:T(8,128)})) %all-reduce.3.cloned.1.call-update) | async-done | bytes 1048592 | tf_op jit(solution)/shard_map/psum | solution.py:77
  235.5 0.7 constant_dynamic-slice_fusion
  236.2 0.2 fusion.5
  236.5 0.2 fusion.7
  236.7 0.5 fusion.23
  237.2 1.2 convolution_add_fusion
  (4 shorter events, 0.0 us)
Async XLA Ops:
  7.2 30.5 %copy-start.4 = (bf16[2,128,512]{2,1,0:T(8,128)(2,1)S(1)}, bf16[2,128,512]{2,1,0:T(8,128)(2,1)}, u32[]{:S(2)}) copy-start(bf16[2,128,512]{2,1,0:T(8,128)(2,1)} %param.5) | copy-start | bytes 786436
  7.2 30.5 %all-gather.5.cloned.1.call-start = ((), (), s32[]{:S(2)}) async-start(), calls=%async_computation | async-start | bytes 1179648 | tf_op jit(solution)/shard_map/all_gather | solution.py:54
  9.0 57.0 %all-gather.7.cloned.1.call-start = ((), (), s32[]{:S(2)}) async-start(), calls=%async_computation.1 | async-start | bytes 1179648 | tf_op jit(solution)/shard_map/all_gather | solution.py:54
  41.7 8.2 %copy-start = (f32[4096,512]{1,0:T(8,128)}, f32[4096,512]{1,0:T(8,128)S(1)}, u32[]{:S(2)}) copy-start(f32[4096,512]{1,0:T(8,128)S(1)} %bitcast_add_fusion) | copy-start | bytes 25165828
  48.1 25.7 %copy-start.2 = (f32[1024,128]{1,0:T(8,128)}, f32[1024,128]{1,0:T(8,128)S(1)}, u32[]{:S(2)}) copy-start(f32[1024,128]{1,0:T(8,128)S(1)} %convolution_multiply_fusion.1) | copy-start | bytes 1572868
  73.8 3.2 %copy-start.1 = (f32[4096,512]{1,0:T(8,128)}, f32[4096,512]{1,0:T(8,128)S(1)}, u32[]{:S(2)}) copy-start(f32[4096,512]{1,0:T(8,128)S(1)} %fusion.2) | copy-start | bytes 25165828
  83.4 1.9 copy-start.3
  85.2 150.3 %all-reduce.3.cloned.1.call-start = ((), (), s32[]{:S(2)}) async-start(), calls=%async_computation.2 | async-start | bytes 2097152 | tf_op jit(solution)/shard_map/psum | solution.py:77
Sparse Core Ops, SparseCore 0:
  9.8 27.8 all-gather.4
  40.1 25.7 all-gather.6
  89.6 145.8 all-reduce.2
where the time goes:
time: 250 us; the launch traced here: 245 us
  waiting for transfers between devices  159 us (64%)
  matrix products  49 us (20%)
  between operations  14 us (6%)
  other arithmetic  13.7 us (5%)
  local copies, waits for them, and re-layouts  9.51 us (4%)
    psum x1, waiting for transfers between devices, shards(): summed = lax.psum(grid, 'dp')  131 us
    all_gather x2, waiting for transfers between devices, shards(): lax.all_gather(inputs[step], 'tensor', axis=1, tiled=True)  26.5 us
    dot_general x4, matrix products, decode_low(): jnp.einsum('ki,rkj->rij', low_rows, wide, precision=lax.Precision.HIGHEST)  20.4 us
    dot_general x2, matrix products, shards(): lax.dot_general(lax.all_gather(inputs[step], 'tensor', axis=1, tiled=True...  11.8 us
    convert_element_type x1, other arithmetic, shards(): new_momentum = state.astype(jnp.bfloat16)[None]  9.45 us
    dot_general x2, matrix products, shards(): jnp.einsum('ki,rij->rkj', low_rows, state.reshape(span_rows, side, out_lo...  9.18 us
  transfers between devices with their start and end apart: 3, of which 3 were waited for; matrix products, arithmetic and copies ran while one was open for 20% of the time, Pallas kernels for 0%

commit v1 on v0

v1 whole, which is shorter than its diff:
```python
import functools
import math

import jax
import jax.numpy as jnp
import numpy as np
from jax import lax
from jax.experimental import pallas as pl
from jax.experimental.pallas import tpu as pltpu
from jax.sharding import PartitionSpec as P

MESH = pl.DeviceIdType.MESH
F32 = jnp.float32
BF16 = jnp.bfloat16
SPAN = 64
LOW = 16
BAND = 8
TOK = 128
ROWS = 4096
COLS = 512
SHARD = 512
STEPS = 2
X = 4
GROUPS = 32
Y = 4
PIECES = 4
PIECE = SHARD // PIECES
CHUNKS = 8
FACTOR = 1.0 / math.sqrt(TOK)


def low_rows():
    freq = np.arange(LOW)[:, None]
    place = np.arange(SPAN)[None, :]
    table = np.sqrt(2.0 / SPAN) * np.cos(math.pi * (2.0 * place + 1.0) * freq / (2.0 * SPAN))
    table[0] /= math.sqrt(2.0)
    return table.astype(np.float32)


def constants():
    low = low_rows()
    enc = np.zeros((LOW, 8, 8, SPAN), np.float32)
    col = np.zeros((8, SPAN, 8, LOW), np.float32)
    for block in range(8):
        enc[:, block, block, :] = low
        col[block, :, block, :] = low.T
    enc = enc.reshape(128, 512)
    col = col.reshape(512, 128)
    return np.concatenate([enc, col.T], axis=0), np.concatenate([enc.T, col], axis=1)


def split(a):
    high = a.astype(BF16)
    low = (a - high.astype(F32)).astype(BF16)
    return high, low


def mm(a, b):
    return jnp.dot(a, b, preferred_element_type=F32)


def kernel(
    x_hbm, d_hbm, m_hbm, band_hbm, flat_hbm, tall_hbm,
    out_ref, upd_ref,
    xin, din, m_ref, band_ref, flat, upright, rowenc, rowdec, colenc, coldec,
    xt, val, colmask, wx, rhs, gm, send, recv, tot,
    load_sem, m_sem, gather_send, gather_recv, sum_send, sum_recv,
):
    dp = lax.axis_index("dp")
    tensor = lax.axis_index("tensor")
    cx = tensor // 2
    core = tensor % 2
    cz = dp // Y
    cy = dp % Y

    def tensor_of(step, other):
        return 2 * ((cx + step) % X) + (core + other) % 2

    mate = tensor_of(0, 1)
    right = tensor_of(1, 0)
    left = tensor_of(X - 1, 0)

    barrier = pltpu.get_barrier_semaphore()
    for peer in (mate, right, left):
        pl.semaphore_signal(barrier, inc=1, device_id=(dp, peer), device_id_type=MESH)

    def greet(i, carry):
        pl.semaphore_signal(
            barrier, inc=1, device_id=((dp + i) % GROUPS, tensor), device_id_type=MESH
        )
        return carry

    lax.fori_loop(1, GROUPS, greet, 0)

    loads = []
    for n, (src, dst) in enumerate(
        [(x_hbm, xin), (tall_hbm, upright), (flat_hbm, flat), (d_hbm, din), (band_hbm, band_ref)]
    ):
        copy = pltpu.make_async_copy(src, dst, load_sem.at[n])
        copy.start()
        loads.append(copy)
    x_load, tall_load, flat_load, d_load, band_load = loads

    def m_copy(q):
        rows = pl.ds(pl.multiple_of(q * SHARD, SHARD), SHARD)
        return pltpu.make_async_copy(m_hbm.at[0, rows, :], m_ref.at[rows, :], m_sem.at[q])

    def start_m(q, carry):
        m_copy(q).start()
        return carry

    lax.fori_loop(0, CHUNKS, start_m, 0)

    own = pl.multiple_of(tensor * SHARD, SHARD)
    x_load.wait()
    for step in range(STEPS):
        xt[pl.ds(own, SHARD), step * TOK:(step + 1) * TOK] = xin[step].T

    pl.semaphore_wait(barrier, 3 + GROUPS - 1)

    def piece_copy(owner, piece, target):
        rows = pl.ds(pl.multiple_of(owner * SHARD + piece * PIECE, PIECE), PIECE)
        return pltpu.make_async_remote_copy(
            src_ref=xt.at[rows, :],
            dst_ref=xt.at[rows, :],
            send_sem=gather_send,
            recv_sem=gather_recv.at[owner * PIECES + piece],
            device_id=(dp, target),
            device_id_type=MESH,
        )

    for piece in range(PIECES):
        flip = (piece + PIECES // 2) % PIECES
        piece_copy(tensor, piece, right).start()
        piece_copy(tensor, flip, left).start()
    for piece in range(PIECES):
        piece_copy(tensor, piece, mate).start()

    tall_load.wait()
    flat_load.wait()
    high, low = split(upright[...])
    rowdec[:, 0:128] = high[:, 0:128]
    rowdec[:, 128:256] = low[:, 0:128]
    colenc[:, 0:128] = high[:, 128:256]
    colenc[:, 128:256] = low[:, 128:256]
    high, low = split(flat[...])
    rowenc[0:128, :] = high[0:128]
    rowenc[128:256, :] = low[0:128]
    coldec[0:128, :] = high[128:256]
    coldec[128:256, :] = high[128:256]
    coldec[256:384, :] = low[128:256]
    d_load.wait()
    hats = []
    for step in range(STEPS):
        both = mm(din[step], colenc[...])
        hats.append((both[:, :128] + both[:, 128:]) * FACTOR)
    table = jnp.concatenate(
        [jnp.concatenate([0.9 * hats[0], hats[0]], axis=1), jnp.concatenate([hats[1], hats[1]], axis=1)], axis=0
    )
    high, low = split(table)
    wx[0:256, :] = high
    wx[256:512, :] = high
    wx[512:768, :] = low
    high, low = split(0.9 * din[0].astype(F32))
    rhs[0:128, :] = high
    rhs[128:256, :] = din[1]
    rhs[256:384, :] = low

    band_load.wait()
    picks = band_ref[...].reshape(128, 64).astype(F32).T.astype(BF16)
    away = lax.broadcasted_iota(jnp.int32, (128, 128), 0) - lax.broadcasted_iota(jnp.int32, (128, 128), 1) // LOW * 16
    for n in range(2 * BAND):
        val[:, n * 128:(n + 1) * 128] = mm(picks, (away == n).astype(F32).astype(BF16))
    place = (lax.broadcasted_iota(jnp.int32, (64, 128), 1) % LOW).astype(F32)
    seen = jnp.zeros((64, 128), F32)
    for k in range(BAND):
        seen = jnp.where(val[:, (BAND + k) * 128:(BAND + k + 1) * 128] == place, 1.0, seen)
    colmask[...] = seen

    def momentum_part(q):
        m_copy(q).wait()
        rows = pl.ds(pl.multiple_of(q * SHARD, SHARD), SHARD)
        tall = mm(rowenc[...], m_ref[rows, :])
        high, low = split(tall[:128] + tall[128:])
        both = mm(jnp.concatenate([high, low], axis=0), colenc[...])
        gm[pl.ds(pl.multiple_of(q * 128, 128), 128), :] = both[:128, :128] + both[128:, :128] + both[:128, 128:]

    def momentum_step(q, carry):
        momentum_part(q)
        return carry

    lax.fori_loop(0, CHUNKS // 2, momentum_step, 0)
    half = PIECES // 2
    for piece in range(half):
        piece_copy(left, piece, right).wait_recv()
        piece_copy(left, piece, right).start()
        piece_copy(right, piece + half, left).wait_recv()
        piece_copy(right, piece + half, left).start()
    for piece in range(half):
        piece_copy(left, piece, mate).start()
        piece_copy(right, piece + half, mate).start()
    lax.fori_loop(CHUNKS // 2, CHUNKS, momentum_step, 0)

    def sum_copy(q, i):
        return pltpu.make_async_remote_copy(
            src_ref=send.at[q, pl.ds(i * 16, 16), :],
            dst_ref=recv.at[dp],
            send_sem=sum_send,
            recv_sem=sum_recv,
            device_id=(q * Y + i, tensor),
            device_id_type=MESH,
        )

    def shard_step(s, carry):
        pair = s // 2
        hop = jnp.where(pair == 1, X - 1, jnp.where(pair == 2, 1, jnp.where(pair == 3, 2, 0)))
        q = tensor_of(hop, s % 2)

        @pl.when(s == 2)
        def _():
            for piece in range(half):
                piece_copy(left, piece + half, mate).wait_recv()
                piece_copy(left, piece + half, mate).start()
                piece_copy(right, piece, mate).wait_recv()
                piece_copy(right, piece, mate).start()

        @pl.when(s == 6)
        def _():
            for piece in range(PIECES):
                piece_copy(q, piece, mate).wait_recv()
                piece_copy(q, piece, mate).start()

        @pl.when(s % 2 == 1)
        def _():
            for piece in range(PIECES):
                piece_copy(q, piece, mate).wait_recv()

        rows = pl.ds(pl.multiple_of(q * SHARD, SHARD), SHARD)
        tall = mm(rowenc[...], xt[rows, :])
        high, low = split(tall[:128] + tall[128:])
        grid = mm(jnp.concatenate([high, low, high], axis=1), wx[...])
        base = gm[pl.ds(pl.multiple_of(q * 128, 128), 128), :]
        grid_a = grid[:, :128] + 0.81 * base
        grid_b = grid[:, 128:] + 0.9 * base

        eight = pl.ds(pl.multiple_of(q * 8, 8), 8)
        mask = colmask[eight, :]
        vals = [val[eight, k * 128:(k + 1) * 128] for k in range(BAND)]
        for k in range(BAND):
            got = grid_b[8 * k:8 * k + 8]
            for f in range(k + 1, k + 9):
                got = jnp.where(vals[k] == f, grid_b[8 * f:8 * f + 8], got)
            send[q, pl.ds(k, 8, stride=8), :] = got * mask
        for i in range(Y):
            @pl.when(q * Y + i != dp)
            def _():
                sum_copy(q, i).start()

        kept = []
        for f in range(LOW):
            hit = jnp.zeros((8, 128), F32)
            for k in range(max(0, f - 8), min(7, f) + 1):
                hit = jnp.where(vals[k] == f, mask, hit)
            kept.append(hit * grid_a[8 * f:8 * f + 8])
        high, low = split(jnp.concatenate(kept, axis=0))
        wide = mm(jnp.concatenate([high, low, high], axis=1), coldec[...]) * (-1.0 / FACTOR)
        high, low = split(wide)
        rhs[384:512, :] = high
        rhs[512:640, :] = low
        rhs[640:768, :] = high
        for part in range(2):
            here = pl.ds(pl.multiple_of(q * SHARD + part * 256, 256), 256)
            feats = xt[here, :]
            dec = rowdec[part * 256:(part + 1) * 256, :]
            left_side = jnp.concatenate([feats, feats[:, :128], dec[:, :128], dec], axis=1)
            change = mm(left_side, rhs[...])
            out_ref[0, here, :] = (0.81 * m_ref[here, :].astype(F32) + FACTOR * change).astype(BF16)
        return carry

    lax.fori_loop(0, CHUNKS, shard_step, 0)

    everyone = recv.at[pl.ds(0, GROUPS - 1)]
    pltpu.make_async_copy(everyone, everyone, sum_recv).wait()
    total = send[cz, pl.ds(pl.multiple_of(cy * 16, 16), 16), :]
    recv[dp] = total
    total = jnp.sum(recv[...], axis=0)
    tot[...] = jnp.zeros((64, 128), F32)
    tot[pl.ds(pl.multiple_of(cy * 16, 16), 16), :] = total
    eight = pl.ds(pl.multiple_of(cz * 8, 8), 8)
    vals = [val[eight, k * 128:(k + 1) * 128] for k in range(BAND)]
    sums = [tot[pl.ds(k, 8, stride=8), :] for k in range(BAND)]
    kept = []
    for f in range(LOW):
        hit = jnp.zeros((8, 128), F32)
        for k in range(max(0, f - 8), min(7, f) + 1):
            hit = jnp.where(vals[k] == f, sums[k], hit)
        kept.append(hit)
    high, low = split(jnp.concatenate(kept, axis=0))
    wide = mm(jnp.concatenate([high, low, high], axis=1), coldec[...])
    high, low = split(wide)
    dec = rowdec[pl.ds(pl.multiple_of(cy * 128, 128), 128), :]
    upd_ref[...] = mm(
        jnp.concatenate([dec[:, :128], dec], axis=1), jnp.concatenate([high, low, high], axis=0)
    )

    everyone_sent = recv.at[pl.ds(0, GROUPS - 1)]
    pltpu.make_async_copy(everyone_sent, everyone_sent, sum_send).wait()
    sent = xt.at[pl.ds(0, 7 * SHARD), :]
    pltpu.make_async_copy(sent, sent, gather_send).wait()


def shards(inputs, out_grads, momentum, band):
    consts = [jnp.asarray(c) for c in constants()]
    band_t = jnp.transpose(band, (1, 2, 3, 0))
    hbm = pl.BlockSpec(memory_space=pltpu.HBM)
    vmem = pl.BlockSpec(memory_space=pltpu.VMEM)
    return pl.pallas_call(
        kernel,
        out_shape=(
            jax.ShapeDtypeStruct(momentum.shape, BF16),
            jax.ShapeDtypeStruct((128, COLS), F32),
        ),
        in_specs=[hbm] * 6,
        out_specs=(vmem, vmem),
        scratch_shapes=[
            pltpu.VMEM((STEPS, TOK, SHARD), BF16),
            pltpu.VMEM((STEPS, TOK, COLS), BF16),
            pltpu.VMEM((ROWS, COLS), BF16),
            pltpu.VMEM((8, 2, 8, 64), jnp.int32),
            pltpu.VMEM((256, 512), F32),
            pltpu.VMEM((512, 256), F32),
            pltpu.VMEM((256, 512), BF16),
            pltpu.VMEM((512, 256), BF16),
            pltpu.VMEM((512, 256), BF16),
            pltpu.VMEM((384, 512), BF16),
            pltpu.VMEM((ROWS, STEPS * TOK), BF16),
            pltpu.VMEM((64, 2048), F32),
            pltpu.VMEM((64, 128), F32),
            pltpu.VMEM((768, 256), BF16),
            pltpu.VMEM((768, COLS), BF16),
            pltpu.VMEM((1024, 128), F32),
            pltpu.VMEM((CHUNKS, 64, 128), F32),
            pltpu.VMEM((GROUPS, 16, 128), F32),
            pltpu.VMEM((64, 128), F32),
            pltpu.SemaphoreType.DMA((5,)),
            pltpu.SemaphoreType.DMA((CHUNKS,)),
            pltpu.SemaphoreType.DMA,
            pltpu.SemaphoreType.DMA((CHUNKS * PIECES,)),
            pltpu.SemaphoreType.DMA,
            pltpu.SemaphoreType.DMA,
        ],
        compiler_params=pltpu.CompilerParams(
            collective_id=0, has_side_effects=True, vmem_limit_bytes=40 * 1024 * 1024
        ),
        name="demo_steps",
    )(inputs, out_grads, momentum, band_t, *consts)


def solution(mesh):
    return jax.shard_map(
        shards,
        mesh=mesh,
        in_specs=(
            P(None, "dp", "tensor"),
            P(None, "dp", "tensor"),
            P("dp", None, "tensor"),
            P(None, "tensor", None, None),
        ),
        out_specs=(P("dp", None, "tensor"), P("dp", "tensor")),
        check_vma=False,
    )
```

time: 250 us -> 44.3 us (0.18); the launches traced: 245 us -> 43.9 us
  waiting for transfers between devices: 159 us -> 0 us
  matrix products: 49 us -> 0 us
  Pallas kernels: 0 us -> 33.6 us
  other arithmetic: 13.7 us -> 0 us
  between operations: 14 us -> 0.65 us
    psum x1 -> x0, waiting for transfers between devices: 131 us -> none  [shards(): summed = lax.psum(grid, 'dp')]
    dot_general x14 -> x0, matrix products: 49 us -> none  [the longest x4 20.4 us: decode_low(): jnp.einsum('ki,rkj->rij', low_rows, wide, precision=lax.Precision.HIGHEST)]
    pallas_call x0 -> x1, Pallas kernels: none -> 33.6 us  [shards(): pl.pallas_call(kernel, out_shape=(jax.ShapeDtypeStruct(momentum.shape, BF...]
    all_gather x2 -> x0, waiting for transfers between devices: 26.5 us -> none  [shards(): lax.all_gather(inputs[step], 'tensor', axis=1, tiled=True)]
    convert_element_type x2 -> x0, other arithmetic: 9.46 us -> none  [the longest x1 9.45 us: shards(): new_momentum = state.astype(jnp.bfloat16)[None]]
    unnamed x10 -> x14, local copies, waits for them, and re-layouts: 3.24 us -> 9.72 us
    reshape x1 -> x0, local copies, waits for them, and re-layouts: 3.24 us -> none  [shards(): jnp.einsum('rck,rcl->rkcl', member[:, :, 0], member[:, :, 1])]
    transpose x2 -> x0, other arithmetic: 3.16 us -> none  [the longest x1 3.09 us: shards(): jnp.einsum('rck,rcl->rkcl', member[:, :, 0], member[:, :, 1])]
  transfers between devices with their start and end apart: 3 -> 0, of which waited for: 3 -> 0; matrix products, arithmetic and copies ran while one was open for 20% -> 0% of each run, Pallas kernels for 0% -> 0%
where the time goes in v1:
time: 44.3 us; the launch traced here: 43.9 us
  Pallas kernels  33.6 us (76%)
  local copies, waits for them, and re-layouts  9.72 us (22%)
  between operations  0.65 us (1%)
    pallas_call x1, Pallas kernels, shards(): pl.pallas_call(kernel, out_shape=(jax.ShapeDtypeStruct(momentum.shape, BF...  33.6 us
    unnamed x14, local copies, waits for them, and re-layouts  9.72 us

profile of v1, /device:TPU:5, one launch (start us, length us, event | category | flops | bytes accessed | tf_op | source)
XLA Modules:
  0.0 43.9 jit_solution(10379944547394149157)
XLA Ops:
  0.6 0.0 copy-start
  0.6 2.2 %copy-done = bf16[1,4096,512]{2,1,0:T(8,128)(2,1)S(1)} copy-done((bf16[1,4096,512]{2,1,0:T(8,128)(2,1)S(1)}, bf16[1,4096,512]{2,1,0:T(8,128)(2,1)}, u32[]{:S(2)}) %copy-start) | copy-done | bytes 4194328
  2.8 0.0 copy-start.1
  2.8 1.0 %copy-done.1 = f32[512,256]{1,0:T(8,128)S(1)} copy-done((f32[512,256]{1,0:T(8,128)S(1)}, f32[512,256]{1,0:T(8,128)}, u32[]{:S(2)}) %copy-start.1) | copy-done | bytes 524312
  3.9 0.0 copy-start.2
  3.9 1.0 %copy-done.2 = f32[256,512]{1,0:T(8,128)S(1)} copy-done((f32[256,512]{1,0:T(8,128)S(1)}, f32[256,512]{1,0:T(8,128)}, u32[]{:S(2)}) %copy-start.2) | copy-done | bytes 524312
  4.9 0.0 copy-start.3
  4.9 0.9 %copy-done.3 = bf16[2,128,512]{2,1,0:T(8,128)(2,1)S(1)} copy-done((bf16[2,128,512]{2,1,0:T(8,128)(2,1)S(1)}, bf16[2,128,512]{2,1,0:T(8,128)(2,1)}, u32[]{:S(2)}) %copy-start.3) | copy-done | bytes 262168
  5.9 0.0 copy-start.4
  5.9 0.9 %copy-done.4 = bf16[2,128,512]{2,1,0:T(8,128)(2,1)S(1)} copy-done((bf16[2,128,512]{2,1,0:T(8,128)(2,1)S(1)}, bf16[2,128,512]{2,1,0:T(8,128)(2,1)}, u32[]{:S(2)}) %copy-start.4) | copy-done | bytes 262168
  6.8 0.0 copy-start.5
  6.8 0.8 %copy-done.5 = s32[64,8,2,8]{0,3,2,1:T(8,128)S(1)} copy-done((s32[64,8,2,8]{0,3,2,1:T(8,128)S(1)}, s32[64,8,2,8]{0,3,2,1:T(8,128)}, u32[]{:S(2)}) %copy-start.5) | copy-done | bytes 32792
  7.6 33.6 %demo_steps.1 = (bf16[1,4096,512]{2,1,0:T(8,128)(2,1)S(1)}, f32[128,512]{1,0:T(8,128)S(1)}) custom-call(bf16[2,128,512]{2,1,0:T(8,128)(2,1)S(1)} %copy-done.3, bf16[2,128,512]{2,1,0:T(8,128)(2,1)S(1)} %copy-done.4, bf16[1,4096,512]{2,1,0:T(8,128)(2,1)S(1)} %copy-done, s32[8,2,8,64]{3,2,1,0:T(8,128)S(1)} %bitcast.1, f32[256,512]{1,0:T(8,128)S(1)} %copy-done.2, ...), custom_call_target="tpu_custom_call" | custom-call | tf_op jit(solution)/shard_map/demo_steps/pallas_call | solution.py:317
  41.2 2.0 %copy.10 = bf16[1,4096,512]{2,1,0:T(8,128)(2,1)} copy(bf16[1,4096,512]{2,1,0:T(8,128)(2,1)S(1)} %get-tuple-element.4) | data formatting | bytes 8388608
  43.2 0.7 %copy.11 = f32[128,512]{1,0:T(8,128)} copy(f32[128,512]{1,0:T(8,128)S(1)} %get-tuple-element.5) | data formatting | bytes 524288
Async XLA Ops:
  0.6 2.2 %copy-start = (bf16[1,4096,512]{2,1,0:T(8,128)(2,1)S(1)}, bf16[1,4096,512]{2,1,0:T(8,128)(2,1)}, u32[]{:S(2)}) copy-start(bf16[1,4096,512]{2,1,0:T(8,128)(2,1)} %m_hbm.1) | copy-start | bytes 12582916
  2.8 1.0 %copy-start.1 = (f32[512,256]{1,0:T(8,128)S(1)}, f32[512,256]{1,0:T(8,128)}, u32[]{:S(2)}) copy-start(f32[512,256]{1,0:T(8,128)} %constant.5.clone.tall_hbm) | copy-start | bytes 1572868
  3.9 1.0 %copy-start.2 = (f32[256,512]{1,0:T(8,128)S(1)}, f32[256,512]{1,0:T(8,128)}, u32[]{:S(2)}) copy-start(f32[256,512]{1,0:T(8,128)} %constant.4.clone.flat_hbm) | copy-start | bytes 1572868
  4.9 0.9 %copy-start.3 = (bf16[2,128,512]{2,1,0:T(8,128)(2,1)S(1)}, bf16[2,128,512]{2,1,0:T(8,128)(2,1)}, u32[]{:S(2)}) copy-start(bf16[2,128,512]{2,1,0:T(8,128)(2,1)} %x_hbm.1) | copy-start | bytes 786436
  5.9 0.9 %copy-start.4 = (bf16[2,128,512]{2,1,0:T(8,128)(2,1)S(1)}, bf16[2,128,512]{2,1,0:T(8,128)(2,1)}, u32[]{:S(2)}) copy-start(bf16[2,128,512]{2,1,0:T(8,128)(2,1)} %d_hbm.1) | copy-start | bytes 786436
  6.8 0.8 %copy-start.5 = (s32[64,8,2,8]{0,3,2,1:T(8,128)S(1)}, s32[64,8,2,8]{0,3,2,1:T(8,128)}, u32[]{:S(2)}) copy-start(s32[64,8,2,8]{0,3,2,1:T(8,128)} %param.9) | copy-start | bytes 98308

commit v2 on v1

v2 whole, which is shorter than its diff:
```python
import functools
import math

import jax
import jax.numpy as jnp
import numpy as np
from jax import lax
from jax.experimental import pallas as pl
from jax.experimental.pallas import tpu as pltpu
from jax.sharding import PartitionSpec as P

MESH = pl.DeviceIdType.MESH
F32 = jnp.float32
BF16 = jnp.bfloat16
SPAN = 64
LOW = 16
BAND = 8
TOK = 128
ROWS = 4096
COLS = 512
SHARD = 512
STEPS = 2
X = 4
GROUPS = 32
Y = 4
HALF = SHARD // 2
CHUNKS = 8
FACTOR = 1.0 / math.sqrt(TOK)


def low_rows():
    freq = np.arange(LOW)[:, None]
    place = np.arange(SPAN)[None, :]
    table = np.sqrt(2.0 / SPAN) * np.cos(math.pi * (2.0 * place + 1.0) * freq / (2.0 * SPAN))
    table[0] /= math.sqrt(2.0)
    return table.astype(np.float32)


def constants():
    low = low_rows()
    enc = np.zeros((LOW, 8, 8, SPAN), np.float32)
    col = np.zeros((8, SPAN, 8, LOW), np.float32)
    for block in range(8):
        enc[:, block, block, :] = low
        col[block, :, block, :] = low.T
    enc = enc.reshape(128, 512)
    col = col.reshape(512, 128)
    return np.concatenate([enc, col.T], axis=0), np.concatenate([enc.T, col], axis=1)


def split(a):
    high = a.astype(BF16)
    low = (a - high.astype(F32)).astype(BF16)
    return high, low


def mm(a, b):
    return jnp.dot(a, b, preferred_element_type=F32)


def kernel(
    x_hbm, d_hbm, m_hbm, band_hbm, flat_hbm, tall_hbm,
    out_ref, upd_ref,
    xin, din, m_ref, band_ref, flat, upright, rowenc, rowdec, colenc, coldec,
    xt, val, colmask, pull, push, wx, rhs, gm, send, recv, tot,
    load_sem, m_sem, gather_send, gather_recv, sum_send, sum_recv,
):
    dp = lax.axis_index("dp")
    tensor = lax.axis_index("tensor")
    cx = tensor // 2
    core = tensor % 2
    cz = dp // Y
    cy = dp % Y

    def tensor_of(hop, other):
        return 2 * ((cx + hop) % X) + (core + other) % 2

    mate = tensor_of(0, 1)
    right = tensor_of(1, 0)
    left = tensor_of(X - 1, 0)
    opposite = tensor_of(2, 0)

    def load(src, dst, n):
        copy = pltpu.make_async_copy(src, dst, load_sem.at[n])
        copy.start()
        return copy

    x_loads = [
        load(x_hbm.at[:, :, half * 256:(half + 1) * 256], xin.at[:, :, half * 256:(half + 1) * 256], half)
        for half in range(2)
    ]
    barrier = pltpu.get_barrier_semaphore()
    for peer in (mate, right, left):
        pl.semaphore_signal(barrier, inc=1, device_id=(dp, peer), device_id_type=MESH)
    tall_load = load(tall_hbm, upright, 2)
    flat_load = load(flat_hbm, flat, 3)
    d_load = load(d_hbm, din, 4)
    band_load = load(band_hbm, band_ref, 5)

    def m_copy(p):
        rows = pl.ds(pl.multiple_of(p * 2 * SHARD, 2 * SHARD), 2 * SHARD)
        return pltpu.make_async_copy(m_hbm.at[0, rows, :], m_ref.at[rows, :], m_sem.at[p])

    for p in range(X):
        m_copy(p).start()

    def greet(i, carry):
        pl.semaphore_signal(
            barrier, inc=1, device_id=((dp + i) % GROUPS, tensor), device_id_type=MESH
        )
        return carry

    lax.fori_loop(1, GROUPS, greet, 0)

    def half_copy(owner, half, target):
        rows = pl.ds(pl.multiple_of(owner * SHARD + half * HALF, HALF), HALF)
        return pltpu.make_async_remote_copy(
            src_ref=xt.at[rows, :],
            dst_ref=xt.at[rows, :],
            send_sem=gather_send,
            recv_sem=gather_recv.at[owner * 2 + half],
            device_id=(dp, target),
            device_id_type=MESH,
        )

    def turn(half):
        x_loads[half].wait()
        rows = pl.ds(pl.multiple_of(tensor * SHARD + half * HALF, HALF), HALF)
        for step in range(STEPS):
            xt[rows, step * TOK:(step + 1) * TOK] = xin[step, :, half * HALF:(half + 1) * HALF].T

    turn(0)
    pl.semaphore_wait(barrier, 3 + GROUPS - 1)
    half_copy(tensor, 0, right).start()
    turn(1)
    half_copy(tensor, 1, left).start()
    half_copy(tensor, 0, mate).start()
    half_copy(tensor, 1, mate).start()
    half_copy(tensor, 1, right).start()
    half_copy(tensor, 0, left).start()

    tall_load.wait()
    flat_load.wait()
    high, low = split(upright[...])
    rowdec[:, 0:128] = high[:, 0:128]
    rowdec[:, 128:256] = low[:, 0:128]
    colenc[:, 0:128] = high[:, 128:256]
    colenc[:, 128:256] = low[:, 128:256]
    high, low = split(flat[...])
    rowenc[0:128, :] = high[0:128]
    rowenc[128:256, :] = low[0:128]
    coldec[0:128, :] = high[128:256]
    coldec[128:256, :] = high[128:256]
    coldec[256:384, :] = low[128:256]
    d_load.wait()
    both = mm(jnp.concatenate([din[0], din[1]], axis=0), colenc[...])
    hats = (both[:, :128] + both[:, 128:]) * FACTOR
    table = jnp.concatenate(
        [jnp.concatenate([0.9 * hats[:128], hats[:128]], axis=1), jnp.concatenate([hats[128:], hats[128:]], axis=1)],
        axis=0,
    )
    high, low = split(table)
    wx[0:256, :] = high
    wx[256:512, :] = high
    wx[512:768, :] = low
    high, low = split(0.9 * din[0].astype(F32))
    for unit in range(2):
        rhs[unit, 0:128, :] = high
        rhs[unit, 128:256, :] = din[1]
        rhs[unit, 256:384, :] = low

    band_load.wait()
    picks = band_ref[...].reshape(128, 64).astype(F32).T.astype(BF16)
    away = lax.broadcasted_iota(jnp.int32, (128, 128), 0) - lax.broadcasted_iota(jnp.int32, (128, 128), 1) // LOW * 16
    for n in range(2 * BAND):
        val[:, n * 128:(n + 1) * 128] = mm(picks, (away == n).astype(F32).astype(BF16))
    place = (lax.broadcasted_iota(jnp.int32, (64, 128), 1) % LOW).astype(F32)
    seen = jnp.zeros((64, 128), F32)
    ahead = jnp.zeros((64, 128), F32)
    back = jnp.full((64, 128), -1.0, F32)
    for k in range(BAND):
        freq = val[:, (BAND + k) * 128:(BAND + k + 1) * 128]
        seen = jnp.where(freq == place, 1.0, seen)
        back = jnp.where(freq == place, place - k, back)
        ahead = jnp.where(place == k, freq - k, ahead)
    colmask[...] = seen
    pull[...] = ahead
    push[...] = back

    def momentum_step(p, carry):
        m_copy(p).wait()
        rows = pl.ds(pl.multiple_of(p * 2 * SHARD, 2 * SHARD), 2 * SHARD)
        thin = mm(m_ref[rows, :], colenc[...])
        high, low = split(thin[:, :128] + thin[:, 128:])
        both = mm(
            rowenc[...], jnp.concatenate([high[:SHARD], low[:SHARD], high[SHARD:], low[SHARD:]], axis=1)
        )
        for unit in range(2):
            at = unit * 256
            gm[2 * p + unit] = both[:128, at:at + 128] + both[:128, at + 128:at + 256] + both[128:, at:at + 128]
        return carry

    lax.fori_loop(0, X, momentum_step, 0)

    top = lax.broadcasted_iota(jnp.int32, (8, 128), 0) < 4
    lane = lax.broadcasted_iota(jnp.int32, (8, 128), 1) % LOW < BAND

    def eight_of(ref, owner):
        return ref[pl.ds(pl.multiple_of(owner * 8, 8), 8), :]

    def pair_step(s, carry):
        hop_a = jnp.where(s == 0, 0, jnp.where(s == 1, X - 1, jnp.where(s == 2, 1, 2)))
        hop_b = jnp.where(s == 0, 0, jnp.where(s == 1, 1, jnp.where(s == 2, X - 1, 2)))
        owners = [(tensor_of(hop_a, other), tensor_of(hop_b, other)) for other in range(2)]

        @pl.when(s > 0)
        def _():
            half_copy(owners[0][0], 0, mate).wait_recv()
            half_copy(owners[0][0], 0, mate).start()

            @pl.when(s == 1)
            def _():
                half_copy(left, 0, right).start()

            half_copy(owners[0][1], 1, mate).wait_recv()
            half_copy(owners[0][1], 1, mate).start()

            @pl.when(s == 1)
            def _():
                half_copy(right, 1, left).start()

        half_copy(owners[1][0], 0, mate).wait_recv()
        half_copy(owners[1][1], 1, mate).wait_recv()

        def half_rows(owner, half):
            return pl.ds(pl.multiple_of(owner * SHARD + half * HALF, HALF), HALF)

        feats = [
            jnp.concatenate([xt[half_rows(a, 0), :], xt[half_rows(b, 1), :]], axis=0) for a, b in owners
        ]
        tall = mm(rowenc[...], jnp.concatenate(feats, axis=1))
        tall = tall[:128] + tall[128:]
        high, low = split(jnp.concatenate([tall[:, :256], tall[:, 256:]], axis=0))
        grid = mm(jnp.concatenate([high, low, high], axis=1), wx[...])

        masked = []
        for unit, (a, b) in enumerate(owners):
            def mixed(ref, cols=slice(None)):
                return jnp.where(top, eight_of(ref, a)[:, cols], eight_of(ref, b)[:, cols])

            mask = mixed(colmask)
            ahead = mixed(pull)
            vals = [
                jnp.where(
                    top,
                    val[pl.ds(pl.multiple_of(a * 8, 8), 8), k * 128:(k + 1) * 128],
                    val[pl.ds(pl.multiple_of(b * 8, 8), 8), k * 128:(k + 1) * 128],
                )
                for k in range(BAND)
            ]
            grid_a, grid_b = [], []
            for f in range(LOW):
                base = jnp.where(top, gm[a, 8 * f:8 * f + 8, :], gm[b, 8 * f:8 * f + 8, :])
                row = unit * 128 + 8 * f
                grid_a.append(grid[row:row + 8, :128] + 0.81 * base)
                grid_b.append(grid[row:row + 8, 128:] + 0.9 * base)
            thin = []
            for k in range(BAND):
                got = grid_b[k]
                for f in range(k + 1, k + 9):
                    got = jnp.where(vals[k] == f, grid_b[f], got)
                moved = got
                for shift in range(1, 9):
                    moved = jnp.where(ahead == shift, pltpu.roll(got, 128 - shift, 1), moved)
                thin.append(moved)
            for k in range(BAND // 2):
                packed = jnp.where(lane, thin[k], pltpu.roll(thin[k + BAND // 2], BAND, 1))
                stage = s * 2 + unit
                send[stage, pl.ds(k, 8, stride=4), :] = packed
            for f in range(LOW):
                hit = jnp.zeros((8, 128), F32)
                for k in range(max(0, f - 8), min(7, f) + 1):
                    hit = jnp.where(vals[k] == f, mask, hit)
                masked.append(hit * grid_a[f])

        for unit, (a, b) in enumerate(owners):
            for i in range(Y):
                owner = a if i < Y // 2 else b
                tile = send.at[s * 2 + unit, pl.ds(i * 8, 8), :]

                @pl.when(owner * Y + i != dp)
                def _():
                    pltpu.make_async_remote_copy(
                        src_ref=tile,
                        dst_ref=recv.at[dp],
                        send_sem=sum_send,
                        recv_sem=sum_recv,
                        device_id=(owner * Y + i, tensor),
                        device_id_type=MESH,
                    ).start()

                @pl.when(owner * Y + i == dp)
                def _():
                    recv[dp] = send[s * 2 + unit, i * 8:(i + 1) * 8, :]

        high, low = split(jnp.concatenate(masked, axis=0))
        wide = mm(jnp.concatenate([high, low, high], axis=1), coldec[...]) * (-1.0 / FACTOR)
        high, low = split(wide)
        for unit, (a, b) in enumerate(owners):
            here = slice(unit * 128, (unit + 1) * 128)
            rhs[unit, 384:512, :] = high[here]
            rhs[unit, 512:640, :] = low[here]
            rhs[unit, 640:768, :] = high[here]
        for unit, (a, b) in enumerate(owners):
            for half, owner in enumerate((a, b)):
                rows = half_rows(owner, half)
                part = xt[rows, :]
                dec = rowdec[half * HALF:(half + 1) * HALF, :]
                left_side = jnp.concatenate([part, part[:, :128], dec[:, :128], dec], axis=1)
                change = mm(left_side, rhs[unit])
                out_ref[0, rows, :] = (0.81 * m_ref[rows, :].astype(F32) + FACTOR * change).astype(BF16)
        return carry

    lax.fori_loop(0, X, pair_step, 0)

    everyone = recv.at[pl.ds(0, GROUPS - 1)]
    pltpu.make_async_copy(everyone, everyone, sum_recv).wait()
    tot[...] = jnp.zeros((32, 128), F32)
    tot[pl.ds(pl.multiple_of(cy * 8, 8), 8), :] = jnp.sum(recv[...], axis=0)
    behind = eight_of(push, cz)
    vals = [val[pl.ds(pl.multiple_of(cz * 8, 8), 8), k * 128:(k + 1) * 128] for k in range(BAND)]
    sums = []
    for part in range(2):
        for k in range(BAND // 2):
            packed = tot[pl.ds(k, 8, stride=4), :]
            if part:
                packed = pltpu.roll(packed, 128 - BAND, 1)
            full = jnp.zeros((8, 128), F32)
            for shift in range(9):
                moved = pltpu.roll(packed, shift, 1) if shift else packed
                full = jnp.where(behind == shift, moved, full)
            sums.append(full)
    kept = []
    for f in range(LOW):
        hit = jnp.zeros((8, 128), F32)
        for k in range(max(0, f - 8), min(7, f) + 1):
            hit = jnp.where(vals[k] == f, sums[k], hit)
        kept.append(hit)
    high, low = split(jnp.concatenate(kept, axis=0))
    wide = mm(jnp.concatenate([high, low, high], axis=1), coldec[...])
    high, low = split(wide)
    dec = rowdec[pl.ds(pl.multiple_of(cy * 128, 128), 128), :]
    upd_ref[...] = mm(
        jnp.concatenate([dec[:, :128], dec], axis=1), jnp.concatenate([high, low, high], axis=0)
    )

    everyone_sent = recv.at[pl.ds(0, GROUPS - 1)]
    pltpu.make_async_copy(everyone_sent, everyone_sent, sum_send).wait()
    sent = xt.at[pl.ds(0, 7 * SHARD), :]
    pltpu.make_async_copy(sent, sent, gather_send).wait()


def shards(inputs, out_grads, momentum, band):
    consts = [jnp.asarray(c) for c in constants()]
    band_t = jnp.transpose(band, (1, 2, 3, 0))
    hbm = pl.BlockSpec(memory_space=pltpu.HBM)
    vmem = pl.BlockSpec(memory_space=pltpu.VMEM)
    return pl.pallas_call(
        kernel,
        out_shape=(
            pltpu.VMEM(momentum.shape, BF16),
            pltpu.VMEM((128, COLS), F32),
        ),
        in_specs=[hbm] * 6,
        out_specs=(vmem, vmem),
        scratch_shapes=[
            pltpu.VMEM((STEPS, TOK, SHARD), BF16),
            pltpu.VMEM((STEPS, TOK, COLS), BF16),
            pltpu.VMEM((ROWS, COLS), BF16),
            pltpu.VMEM((8, 2, 8, 64), jnp.int32),
            pltpu.VMEM((256, 512), F32),
            pltpu.VMEM((512, 256), F32),
            pltpu.VMEM((256, 512), BF16),
            pltpu.VMEM((512, 256), BF16),
            pltpu.VMEM((512, 256), BF16),
            pltpu.VMEM((384, 512), BF16),
            pltpu.VMEM((ROWS, STEPS * TOK), BF16),
            pltpu.VMEM((64, 2048), F32),
            pltpu.VMEM((64, 128), F32),
            pltpu.VMEM((64, 128), F32),
            pltpu.VMEM((64, 128), F32),
            pltpu.VMEM((768, 256), BF16),
            pltpu.VMEM((2, 768, COLS), BF16),
            pltpu.VMEM((CHUNKS, 128, 128), F32),
            pltpu.VMEM((CHUNKS, 32, 128), F32),
            pltpu.VMEM((GROUPS, 8, 128), F32),
            pltpu.VMEM((32, 128), F32),
            pltpu.SemaphoreType.DMA((6,)),
            pltpu.SemaphoreType.DMA((X,)),
            pltpu.SemaphoreType.DMA,
            pltpu.SemaphoreType.DMA((CHUNKS * 2,)),
            pltpu.SemaphoreType.DMA,
            pltpu.SemaphoreType.DMA,
        ],
        compiler_params=pltpu.CompilerParams(
            collective_id=0, has_side_effects=True, vmem_limit_bytes=40 * 1024 * 1024
        ),
        name="demo_steps",
    )(*[pltpu.with_memory_space_constraint(a, pltpu.HBM) for a in (inputs, out_grads, momentum, band_t, *consts)])


def solution(mesh):
    return jax.shard_map(
        shards,
        mesh=mesh,
        in_specs=(
            P(None, "dp", "tensor"),
            P(None, "dp", "tensor"),
            P("dp", None, "tensor"),
            P(None, "tensor", None, None),
        ),
        out_specs=(P("dp", None, "tensor"), P("dp", "tensor")),
        check_vma=False,
    )
```

time: 44.3 us -> 34.4 us (0.78)
  local copies, waits for them, and re-layouts: 9.72 us -> 2.72 us
  Pallas kernels: 33.6 us -> 30.9 us
    unnamed x14 -> x2, local copies, waits for them, and re-layouts: 9.72 us -> 2.72 us
    pallas_call x1, Pallas kernels: 33.6 us -> 30.9 us  [shards(): pl.pallas_call(kernel, out_shape=(pltpu.VMEM(momentum.shape, BF16), pltpu...]
where the time goes in v2:
time: 34.4 us; the launch traced here: 34.3 us
  Pallas kernels  30.9 us (90%)
  local copies, waits for them, and re-layouts  2.72 us (8%)
  between operations  0.64 us (2%)
    pallas_call x1, Pallas kernels, shards(): pl.pallas_call(kernel, out_shape=(pltpu.VMEM(momentum.shape, BF16), pltpu...  30.9 us
    unnamed x2, local copies, waits for them, and re-layouts  2.72 us

profile of v2, /device:TPU:5, one launch (start us, length us, event | category | flops | bytes accessed | tf_op | source)
XLA Modules:
  0.0 34.3 jit_solution(15156110458028171292)
XLA Ops:
  0.6 30.9 %demo_steps.1 = (bf16[1,4096,512]{2,1,0:T(8,128)(2,1)S(1)}, f32[128,512]{1,0:T(8,128)S(1)}) custom-call(bf16[2,128,512]{2,1,0:T(8,128)(2,1)} %x_hbm.1, bf16[2,128,512]{2,1,0:T(8,128)(2,1)} %d_hbm.1, bf16[1,4096,512]{2,1,0:T(8,128)(2,1)} %m_hbm.1, s32[8,2,8,64]{3,2,1,0:T(8,128)} %bitcast.1, f32[256,512]{1,0:T(8,128)} %constant.4.clone.flat_hbm, ...), custom_call_target="tpu_custom_call" | custom-call | tf_op jit(solution)/shard_map/demo_steps/pallas_call | solution.py:368
  31.6 2.0 %copy.10 = bf16[1,4096,512]{2,1,0:T(8,128)(2,1)} copy(bf16[1,4096,512]{2,1,0:T(8,128)(2,1)S(1)} %get-tuple-element.2) | data formatting | bytes 8388608
  33.6 0.7 %copy.11 = f32[128,512]{1,0:T(8,128)} copy(f32[128,512]{1,0:T(8,128)S(1)} %get-tuple-element.3) | data formatting | bytes 524288

commit v3 on v2

--- a/solution.py
+++ b/solution.py
@@ -3,6 +3,7 @@
 
 import jax
 import jax.numpy as jnp
+import ml_dtypes
 import numpy as np
 from jax import lax
 from jax.experimental import pallas as pl
@@ -25,7 +26,13 @@
 Y = 4
 HALF = SHARD // 2
 CHUNKS = 8
+PARTS = 8
 FACTOR = 1.0 / math.sqrt(TOK)
+
+
+def split_const(table):
+    high = table.astype(ml_dtypes.bfloat16).astype(np.float32)
+    return high, (table - high).astype(ml_dtypes.bfloat16).astype(np.float32)
 
 
 def low_rows():
@@ -38,14 +45,23 @@
 
 def constants():
     low = low_rows()
+    four = np.zeros((LOW, 4, 4, SPAN), np.float32)
     enc = np.zeros((LOW, 8, 8, SPAN), np.float32)
     col = np.zeros((8, SPAN, 8, LOW), np.float32)
     for block in range(8):
         enc[:, block, block, :] = low
         col[block, :, block, :] = low.T
-    enc = enc.reshape(128, 512)
-    col = col.reshape(512, 128)
-    return np.concatenate([enc, col.T], axis=0), np.concatenate([enc.T, col], axis=1)
+        if block < 4:
+            four[:, block, block, :] = low
+    rowenc = np.concatenate(split_const(four.reshape(64, 256)), axis=0)
+    rowdec = np.concatenate(split_const(enc.reshape(128, 512).T), axis=1)
+    colenc = np.concatenate(split_const(col.reshape(512, 128)), axis=1)
+    high, lower = split_const(col.reshape(512, 128).T)
+    zero = np.zeros((64, 256), np.float32)
+    first = [high[:64, :256], lower[:64, :256], high[:64, :256], zero]
+    second = [lower[64:, 256:], high[64:, 256:], zero, high[64:, 256:]]
+    coldec = np.concatenate([np.concatenate(first, axis=0), np.concatenate(second, axis=0)], axis=1)
+    return rowenc, rowdec, colenc, coldec
 
 
 def split(a):
@@ -58,11 +74,20 @@
     return jnp.dot(a, b, preferred_element_type=F32)
 
 
+def widen(grids, coldec):
+    lane = lax.broadcasted_iota(jnp.int32, grids.shape, 1) < 64
+    turned = pltpu.roll(grids, 64, 1)
+    high, low = split(grids)
+    first = jnp.concatenate([jnp.where(lane, grids, turned).astype(BF16), low], axis=1)
+    second = jnp.concatenate([jnp.where(lane, turned, grids).astype(BF16), low], axis=1)
+    return jnp.concatenate([mm(first, coldec[:, :256]), mm(second, coldec[:, 256:])], axis=1)
+
+
 def kernel(
-    x_hbm, d_hbm, m_hbm, band_hbm, flat_hbm, tall_hbm,
-    out_ref, upd_ref,
-    xin, din, m_ref, band_ref, flat, upright, rowenc, rowdec, colenc, coldec,
-    xt, val, colmask, pull, push, wx, rhs, gm, send, recv, tot,
+    x_hbm, d_hbm, m_hbm, band_hbm, rowenc_hbm, rowdec_hbm, colenc_hbm, coldec_hbm,
+    out_ref, recv, own, coldec, rowdec,
+    xin, din, m_ref, band_ref, rowenc_in, rowdec_in, colenc_in, coldec_in, rowenc, colenc,
+    xt, val, colmask, pull, push, wx, rhs, gm, kept, send,
     load_sem, m_sem, gather_send, gather_recv, sum_send, sum_recv,
 ):
     dp = lax.axis_index("dp")
@@ -78,7 +103,6 @@
     mate = tensor_of(0, 1)
     right = tensor_of(1, 0)
     left = tensor_of(X - 1, 0)
-    opposite = tensor_of(2, 0)
 
     def load(src, dst, n):
         copy = pltpu.make_async_copy(src, dst, load_sem.at[n])
@@ -92,10 +116,12 @@
     barrier = pltpu.get_barrier_semaphore()
     for peer in (mate, right, left):
         pl.semaphore_signal(barrier, inc=1, device_id=(dp, peer), device_id_type=MESH)
-    tall_load = load(tall_hbm, upright, 2)
-    flat_load = load(flat_hbm, flat, 3)
-    d_load = load(d_hbm, din, 4)
-    band_load = load(band_hbm, band_ref, 5)
+    colenc_load = load(colenc_hbm, colenc_in, 2)
+    d_load = load(d_hbm, din, 3)
+    band_load = load(band_hbm, band_ref, 4)
+    rowenc_load = load(rowenc_hbm, rowenc_in, 5)
+    coldec_load = load(coldec_hbm, coldec_in, 6)
+    rowdec_load = load(rowdec_hbm, rowdec_in, 7)
 
     def m_copy(p):
         rows = pl.ds(pl.multiple_of(p * 2 * SHARD, 2 * SHARD), 2 * SHARD)
@@ -139,19 +165,8 @@
     half_copy(tensor, 1, right).start()
     half_copy(tensor, 0, left).start()
 
-    tall_load.wait()
-    flat_load.wait()
-    high, low = split(upright[...])
-    rowdec[:, 0:128] = high[:, 0:128]
-    rowdec[:, 128:256] = low[:, 0:128]
-    colenc[:, 0:128] = high[:, 128:256]
-    colenc[:, 128:256] = low[:, 128:256]
-    high, low = split(flat[...])
-    rowenc[0:128, :] = high[0:128]
-    rowenc[128:256, :] = low[0:128]
-    coldec[0:128, :] = high[128:256]
-    coldec[128:256, :] = high[128:256]
-    coldec[256:384, :] = low[128:256]
+    colenc_load.wait()
+    colenc[...] = colenc_in[...].astype(BF16)
     d_load.wait()
     both = mm(jnp.concatenate([din[0], din[1]], axis=0), colenc[...])
     hats = (both[:, :128] + both[:, 128:]) * FACTOR
@@ -187,20 +202,29 @@
     pull[...] = ahead
     push[...] = back
 
+    rowenc_load.wait()
+    rowenc[...] = rowenc_in[...].astype(BF16)
+
+    def encode(halves):
+        wide = mm(rowenc[...], jnp.concatenate(halves, axis=1))
+        wide = wide[:64] + wide[64:]
+        size = halves[0].shape[1]
+        return split(jnp.concatenate([wide[:, n * size:(n + 1) * size] for n in range(len(halves))], axis=0))
+
     def momentum_step(p, carry):
         m_copy(p).wait()
-        rows = pl.ds(pl.multiple_of(p * 2 * SHARD, 2 * SHARD), 2 * SHARD)
-        thin = mm(m_ref[rows, :], colenc[...])
-        high, low = split(thin[:, :128] + thin[:, 128:])
-        both = mm(
-            rowenc[...], jnp.concatenate([high[:SHARD], low[:SHARD], high[SHARD:], low[SHARD:]], axis=1)
+        high, low = encode(
+            [m_ref[pl.ds(pl.multiple_of(p * 2 * SHARD + n * HALF, HALF), HALF), :] for n in range(4)]
         )
-        for unit in range(2):
-            at = unit * 256
-            gm[2 * p + unit] = both[:128, at:at + 128] + both[:128, at + 128:at + 256] + both[128:, at:at + 128]
+        both = mm(jnp.concatenate([high, low], axis=0), colenc[...])
+        gm[p] = both[:256, :128] + both[:256, 128:] + both[256:, :128]
         return carry
 
     lax.fori_loop(0, X, momentum_step, 0)
+    coldec_load.wait()
+    coldec[...] = coldec_in[...].astype(BF16)
+    rowdec_load.wait()
+    rowdec[...] = rowdec_in[...].astype(BF16)
 
     top = lax.broadcasted_iota(jnp.int32, (8, 128), 0) < 4
     lane = lax.broadcasted_iota(jnp.int32, (8, 128), 1) % LOW < BAND
@@ -208,10 +232,34 @@
     def eight_of(ref, owner):
         return ref[pl.ds(pl.multiple_of(owner * 8, 8), 8), :]
 
-    def pair_step(s, carry):
+    def owners_of(s):
         hop_a = jnp.where(s == 0, 0, jnp.where(s == 1, X - 1, jnp.where(s == 2, 1, 2)))
         hop_b = jnp.where(s == 0, 0, jnp.where(s == 1, 1, jnp.where(s == 2, X - 1, 2)))
-        owners = [(tensor_of(hop_a, other), tensor_of(hop_b, other)) for other in range(2)]
+        return [(tensor_of(hop_a, other), tensor_of(hop_b, other)) for other in range(2)]
+
+    def half_rows(owner, half):
+        return pl.ds(pl.multiple_of(owner * SHARD + half * HALF, HALF), HALF)
+
+    def write_pair(s):
+        grids = jnp.concatenate([kept[s * 2], kept[s * 2 + 1]], axis=0)
+        wide = widen(grids, coldec[...]) * (-1.0 / FACTOR)
+        high, low = split(wide)
+        for unit, (a, b) in enumerate(owners_of(s)):
+            here = slice(unit * 128, (unit + 1) * 128)
+            rhs[unit, 384:512, :] = high[here]
+            rhs[unit, 512:640, :] = low[here]
+            rhs[unit, 640:768, :] = high[here]
+        for unit, (a, b) in enumerate(owners_of(s)):
+            for half, owner in enumerate((a, b)):
+                rows = half_rows(owner, half)
+                part = xt[rows, :]
+                dec = rowdec[half * HALF:(half + 1) * HALF, :]
+                left_side = jnp.concatenate([part, part[:, :128], dec[:, :128], dec], axis=1)
+                change = mm(left_side, rhs[unit])
+                out_ref[0, rows, :] = (0.81 * m_ref[rows, :].astype(F32) + FACTOR * change).astype(BF16)
+
+    def pair_step(s, carry):
+        owners = owners_of(s)
 
         @pl.when(s > 0)
         def _():
@@ -229,21 +277,29 @@
             def _():
                 half_copy(right, 1, left).start()
 
+            write_pair(s - 1)
+
         half_copy(owners[1][0], 0, mate).wait_recv()
         half_copy(owners[1][1], 1, mate).wait_recv()
 
-        def half_rows(owner, half):
-            return pl.ds(pl.multiple_of(owner * SHARD + half * HALF, HALF), HALF)
-
-        feats = [
-            jnp.concatenate([xt[half_rows(a, 0), :], xt[half_rows(b, 1), :]], axis=0) for a, b in owners
-        ]
-        tall = mm(rowenc[...], jnp.concatenate(feats, axis=1))
-        tall = tall[:128] + tall[128:]
-        high, low = split(jnp.concatenate([tall[:, :256], tall[:, 256:]], axis=0))
+        quarters = [(a, 0) if half == 0 else (b, 1) for a, b in owners for half in range(2)]
+        high, low = encode([xt[half_rows(owner, half), :] for owner, half in quarters])
         grid = mm(jnp.concatenate([high, low, high], axis=1), wx[...])
-
-        masked = []
+        grid_a, grid_b = [], []
+        for n, (owner, half) in enumerate(quarters):
+            start = pl.multiple_of((owner % 2) * 128 + half * 64, 64)
+            base = gm[owner // 2, pl.ds(start, 64), :]
+            grid_a.append(grid[n * 64:(n + 1) * 64, :128] + 0.81 * base)
+            grid_b.append(grid[n * 64:(n + 1) * 64, 128:] + 0.9 * base)
+
+        def by_frequency(first, second):
+            tiles = []
+            for n in range(LOW // 2):
+                one, two = first[8 * n:8 * n + 8], second[8 * n:8 * n + 8]
+                tiles.append(jnp.where(top, one, pltpu.roll(two, 4, 0)))
+                tiles.append(jnp.where(top, pltpu.roll(one, 4, 0), two))
+            return tiles
+
         for unit, (a, b) in enumerate(owners):
             def mixed(ref, cols=slice(None)):
                 return jnp.where(top, eight_of(ref, a)[:, cols], eight_of(ref, b)[:, cols])
@@ -258,17 +314,13 @@
                 )
                 for k in range(BAND)
             ]
-            grid_a, grid_b = [], []
-            for f in range(LOW):
-                base = jnp.where(top, gm[a, 8 * f:8 * f + 8, :], gm[b, 8 * f:8 * f + 8, :])
-                row = unit * 128 + 8 * f
-                grid_a.append(grid[row:row + 8, :128] + 0.81 * base)
-                grid_b.append(grid[row:row + 8, 128:] + 0.9 * base)
+            for_a = by_frequency(grid_a[2 * unit], grid_a[2 * unit + 1])
+            for_b = by_frequency(grid_b[2 * unit], grid_b[2 * unit + 1])
             thin = []
             for k in range(BAND):
-                got = grid_b[k]
+                got = for_b[k]
                 for f in range(k + 1, k + 9):
-                    got = jnp.where(vals[k] == f, grid_b[f], got)
+                    got = jnp.where(vals[k] == f, for_b[f], got)
                 moved = got
                 for shift in range(1, 9):
                     moved = jnp.where(ahead == shift, pltpu.roll(got, 128 - shift, 1), moved)
@@ -281,7 +333,7 @@
                 hit = jnp.zeros((8, 128), F32)
                 for k in range(max(0, f - 8), min(7, f) + 1):
                     hit = jnp.where(vals[k] == f, mask, hit)
-                masked.append(hit * grid_a[f])
+                kept[s * 2 + unit, 8 * f:8 * f + 8, :] = hit * for_a[f]
 
         for unit, (a, b) in enumerate(owners):
             for i in range(Y):
@@ -303,32 +355,37 @@
                 def _():
                     recv[dp] = send[s * 2 + unit, i * 8:(i + 1) * 8, :]
 
-        high, low = split(jnp.concatenate(masked, axis=0))
-        wide = mm(jnp.concatenate([high, low, high], axis=1), coldec[...]) * (-1.0 / FACTOR)
-        high, low = split(wide)
-        for unit, (a, b) in enumerate(owners):
-            here = slice(unit * 128, (unit + 1) * 128)
-            rhs[unit, 384:512, :] = high[here]
-            rhs[unit, 512:640, :] = low[here]
-            rhs[unit, 640:768, :] = high[here]
-        for unit, (a, b) in enumerate(owners):
-            for half, owner in enumerate((a, b)):
-                rows = half_rows(owner, half)
-                part = xt[rows, :]
-                dec = rowdec[half * HALF:(half + 1) * HALF, :]
-                left_side = jnp.concatenate([part, part[:, :128], dec[:, :128], dec], axis=1)
-                change = mm(left_side, rhs[unit])
-                out_ref[0, rows, :] = (0.81 * m_ref[rows, :].astype(F32) + FACTOR * change).astype(BF16)
         return carry
 
     lax.fori_loop(0, X, pair_step, 0)
-
+    write_pair(X - 1)
+
+    for k in range(BAND):
+        own[k] = val[pl.ds(pl.multiple_of(cz * 8, 8), 8), k * 128:(k + 1) * 128]
+    own[BAND] = eight_of(push, cz)
     everyone = recv.at[pl.ds(0, GROUPS - 1)]
     pltpu.make_async_copy(everyone, everyone, sum_recv).wait()
+    everyone_sent = recv.at[pl.ds(0, GROUPS - 1)]
+    pltpu.make_async_copy(everyone_sent, everyone_sent, sum_send).wait()
+    sent = xt.at[pl.ds(0, 7 * SHARD), :]
+    pltpu.make_async_copy(sent, sent, gather_send).wait()
+
+
+def finish(new_ref, recv, own, coldec, rowdec, out_hbm, upd_hbm, tot, upd, sem):
+    cy = lax.axis_index("dp") % Y
+    rows = ROWS // PARTS
+    copies = [
+        pltpu.make_async_copy(
+            new_ref.at[0, pl.ds(n * rows, rows), :], out_hbm.at[0, pl.ds(n * rows, rows), :], sem.at[n]
+        )
+        for n in range(PARTS)
+    ]
+    for copy in copies:
+        copy.start()
     tot[...] = jnp.zeros((32, 128), F32)
     tot[pl.ds(pl.multiple_of(cy * 8, 8), 8), :] = jnp.sum(recv[...], axis=0)
-    behind = eight_of(push, cz)
-    vals = [val[pl.ds(pl.multiple_of(cz * 8, 8), 8), k * 128:(k + 1) * 128] for k in range(BAND)]
+    behind = own[BAND]
+    vals = [own[k] for k in range(BAND)]
     sums = []
     for part in range(2):
         for k in range(BAND // 2):
@@ -346,18 +403,18 @@
         for k in range(max(0, f - 8), min(7, f) + 1):
             hit = jnp.where(vals[k] == f, sums[k], hit)
         kept.append(hit)
-    high, low = split(jnp.concatenate(kept, axis=0))
-    wide = mm(jnp.concatenate([high, low, high], axis=1), coldec[...])
+    wide = widen(jnp.concatenate(kept, axis=0), coldec[...])
     high, low = split(wide)
     dec = rowdec[pl.ds(pl.multiple_of(cy * 128, 128), 128), :]
-    upd_ref[...] = mm(
+    upd[...] = mm(
         jnp.concatenate([dec[:, :128], dec], axis=1), jnp.concatenate([high, low, high], axis=0)
     )
 
-    everyone_sent = recv.at[pl.ds(0, GROUPS - 1)]
-    pltpu.make_async_copy(everyone_sent, everyone_sent, sum_send).wait()
-    sent = xt.at[pl.ds(0, 7 * SHARD), :]
-    pltpu.make_async_copy(sent, sent, gather_send).wait()
+    last = pltpu.make_async_copy(upd, upd_hbm, sem.at[PARTS])
+    last.start()
+    for copy in copies:
+        copy.wait()
+    last.wait()
 
 
 def shards(inputs, out_grads, momentum, band):
@@ -365,25 +422,28 @@
     band_t = jnp.transpose(band, (1, 2, 3, 0))
     hbm = pl.BlockSpec(memory_space=pltpu.HBM)
     vmem = pl.BlockSpec(memory_space=pltpu.VMEM)
-    return pl.pallas_call(
+    parts = pl.pallas_call(
         kernel,
         out_shape=(
             pltpu.VMEM(momentum.shape, BF16),
-            pltpu.VMEM((128, COLS), F32),
+            pltpu.VMEM((GROUPS, 8, 128), F32),
+            pltpu.VMEM((BAND + 1, 8, 128), F32),
+            pltpu.VMEM((256, COLS), BF16),
+            pltpu.VMEM((SHARD, 256), BF16),
         ),
-        in_specs=[hbm] * 6,
-        out_specs=(vmem, vmem),
+        in_specs=[hbm] * 8,
+        out_specs=(vmem,) * 5,
         scratch_shapes=[
             pltpu.VMEM((STEPS, TOK, SHARD), BF16),
             pltpu.VMEM((STEPS, TOK, COLS), BF16),
             pltpu.VMEM((ROWS, COLS), BF16),
             pltpu.VMEM((8, 2, 8, 64), jnp.int32),
+            pltpu.VMEM((128, 256), F32),
+            pltpu.VMEM((512, 256), F32),
+            pltpu.VMEM((512, 256), F32),
             pltpu.VMEM((256, 512), F32),
-            pltpu.VMEM((512, 256), F32),
-            pltpu.VMEM((256, 512), BF16),
+            pltpu.VMEM((128, 256), BF16),
             pltpu.VMEM((512, 256), BF16),
-            pltpu.VMEM((512, 256), BF16),
-            pltpu.VMEM((384, 512), BF16),
             pltpu.VMEM((ROWS, STEPS * TOK), BF16),
             pltpu.VMEM((64, 2048), F32),
             pltpu.VMEM((64, 128), F32),
@@ -391,11 +451,10 @@
             pltpu.VMEM((64, 128), F32),
             pltpu.VMEM((768, 256), BF16),
             pltpu.VMEM((2, 768, COLS), BF16),
+            pltpu.VMEM((X, 256, 128), F32),
             pltpu.VMEM((CHUNKS, 128, 128), F32),
             pltpu.VMEM((CHUNKS, 32, 128), F32),
-            pltpu.VMEM((GROUPS, 8, 128), F32),
-            pltpu.VMEM((32, 128), F32),
-            pltpu.SemaphoreType.DMA((6,)),
+            pltpu.SemaphoreType.DMA((8,)),
             pltpu.SemaphoreType.DMA((X,)),
             pltpu.SemaphoreType.DMA,
             pltpu.SemaphoreType.DMA((CHUNKS * 2,)),
@@ -407,6 +466,20 @@
         ),
         name="demo_steps",
     )(*[pltpu.with_memory_space_constraint(a, pltpu.HBM) for a in (inputs, out_grads, momentum, band_t, *consts)])
+    parts = [pltpu.with_memory_space_constraint(a, pltpu.VMEM) for a in parts]
+    return pl.pallas_call(
+        finish,
+        out_shape=(pltpu.HBM(momentum.shape, BF16), pltpu.HBM((128, COLS), F32)),
+        in_specs=[vmem] * 5,
+        out_specs=(hbm, hbm),
+        scratch_shapes=[
+            pltpu.VMEM((32, 128), F32),
+            pltpu.VMEM((128, COLS), F32),
+            pltpu.SemaphoreType.DMA((PARTS + 1,)),
+        ],
+        compiler_params=pltpu.CompilerParams(vmem_limit_bytes=8 * 1024 * 1024),
+        name="demo_finish",
+    )(*parts)
 
 
 def solution(mesh):

time: 34.4 us -> 30.9 us (0.90)
  local copies, waits for them, and re-layouts: 2.72 us -> 0 us
  Pallas kernels: 30.9 us -> 30.2 us
    pallas_call x1, Pallas kernels: 30.9 us -> 27.8 us  [shards(): pl.pallas_call(kernel, out_shape=(pltpu.VMEM(momentum.shape, BF16), pltpu...]
    unnamed x2 -> x0, local copies, waits for them, and re-layouts: 2.72 us -> none
    pallas_call x0 -> x1, Pallas kernels: none -> 2.45 us  [shards(): pl.pallas_call(finish, out_shape=(pltpu.HBM(momentum.shape, BF16), pltpu....]
where the time goes in v3:
time: 30.9 us
  Pallas kernels  30.2 us (98%)
  between operations  0.64 us (2%)
    pallas_call x1, Pallas kernels, shards(): pl.pallas_call(kernel, out_shape=(pltpu.VMEM(momentum.shape, BF16), pltpu...  27.8 us
    pallas_call x1, Pallas kernels, shards(): pl.pallas_call(finish, out_shape=(pltpu.HBM(momentum.shape, BF16), pltpu....  2.45 us

profile of v3, /device:TPU:5, one launch (start us, length us, event | category | flops | bytes accessed | tf_op | source)
XLA Modules:
  0.0 30.9 jit_solution(13161272363581461598)
XLA Ops:
  0.6 27.8 %demo_steps.1 = (bf16[1,4096,512]{2,1,0:T(8,128)(2,1)S(1)}, f32[32,8,128]{2,1,0:T(8,128)S(1)}, f32[9,8,128]{2,1,0:T(8,128)S(1)}, bf16[256,512]{1,0:T(8,128)(2,1)S(1)}, bf16[512,256]{1,0:T(8,128)(2,1)S(1)}) custom-call(bf16[2,128,512]{2,1,0:T(8,128)(2,1)} %x_hbm.1, bf16[2,128,512]{2,1,0:T(8,128)(2,1)} %d_hbm.1, bf16[1,4096,512]{2,1,0:T(8,128)(2,1)} %m_hbm.1, ...), custom_call_target="tpu_custom_call" | custom-call | tf_op jit(solution)/shard_map/demo_steps/pallas_call | solution.py:425
  28.4 2.5 %demo_finish.1 = (bf16[1,4096,512]{2,1,0:T(8,128)(2,1)}, f32[128,512]{1,0:T(8,128)}) custom-call(bf16[1,4096,512]{2,1,0:T(8,128)(2,1)S(1)} %get-tuple-element.7.new_ref, f32[32,8,128]{2,1,0:T(8,128)S(1)} %get-tuple-element.8.recv, f32[9,8,128]{2,1,0:T(8,128)S(1)} %get-tuple-element.9.own, bf16[256,512]{1,0:T(8,128)(2,1)S(1)} %get-tuple-element.10.coldec, ...), custom_call_target="tpu_custom_call" | custom-call | tf_op jit(solution)/shard_map/demo_finish/pallas_call | solution.py:470

commit v4 on v3

--- a/solution.py
+++ b/solution.py
@@ -87,8 +87,8 @@
     x_hbm, d_hbm, m_hbm, band_hbm, rowenc_hbm, rowdec_hbm, colenc_hbm, coldec_hbm,
     out_ref, recv, own, coldec, rowdec,
     xin, din, m_ref, band_ref, rowenc_in, rowdec_in, colenc_in, coldec_in, rowenc, colenc,
-    xt, val, colmask, pull, push, wx, rhs, gm, kept, send,
-    load_sem, m_sem, gather_send, gather_recv, sum_send, sum_recv,
+    xt, val, colmask, pull, push, wx, rhs, gm, kept, send, gm_mate, val_mate, pull_mate, mask_mate,
+    load_sem, m_sem, gather_send, gather_recv, sum_send, sum_recv, swap_send, swap_recv,
 ):
     dp = lax.axis_index("dp")
     tensor = lax.axis_index("tensor")
@@ -103,6 +103,9 @@
     mate = tensor_of(0, 1)
     right = tensor_of(1, 0)
     left = tensor_of(X - 1, 0)
+    far = tensor_of(2, 0)
+    far_mate = tensor_of(2, 1)
+    crossed = cz == far_mate
 
     def load(src, dst, n):
         copy = pltpu.make_async_copy(src, dst, load_sem.at[n])
@@ -138,6 +141,16 @@
 
     lax.fori_loop(1, GROUPS, greet, 0)
 
+    @pl.when(crossed)
+    def _():
+        def greet_mates(i, carry):
+            pl.semaphore_signal(
+                barrier, inc=1, device_id=((dp + i) % GROUPS, mate), device_id_type=MESH
+            )
+            return carry
+
+        lax.fori_loop(1, GROUPS, greet_mates, 0)
+
     def half_copy(owner, half, target):
         rows = pl.ds(pl.multiple_of(owner * SHARD + half * HALF, HALF), HALF)
         return pltpu.make_async_remote_copy(
@@ -156,7 +169,7 @@
             xt[rows, step * TOK:(step + 1) * TOK] = xin[step, :, half * HALF:(half + 1) * HALF].T
 
     turn(0)
-    pl.semaphore_wait(barrier, 3 + GROUPS - 1)
+    pl.semaphore_wait(barrier, 3 + GROUPS - 1 + jnp.where(cz == far, Y - 1, Y))
     half_copy(tensor, 0, right).start()
     turn(1)
     half_copy(tensor, 1, left).start()
@@ -175,9 +188,9 @@
         axis=0,
     )
     high, low = split(table)
-    wx[0:256, :] = high
-    wx[256:512, :] = high
-    wx[512:768, :] = low
+    wx[0:256, 0:256] = high
+    wx[256:512, 0:256] = high
+    wx[512:768, 0:256] = low
     high, low = split(0.9 * din[0].astype(F32))
     for unit in range(2):
         rhs[unit, 0:128, :] = high
@@ -221,6 +234,23 @@
         return carry
 
     lax.fori_loop(0, X, momentum_step, 0)
+
+    def swap(src, dst, n):
+        return pltpu.make_async_remote_copy(
+            src_ref=src, dst_ref=dst, send_sem=swap_send.at[n], recv_sem=swap_recv.at[n],
+            device_id=(dp, mate), device_id_type=MESH,
+        )
+
+    mate_rows = pl.ds(pl.multiple_of(far_mate * 8, 8), 8)
+    swaps = [
+        swap(wx.at[:, 128:256], wx.at[:, 256:384], 0),
+        swap(gm.at[far_mate // 2, pl.ds(pl.multiple_of(far_mate % 2 * 128, 128), 128), :], gm_mate, 1),
+        swap(val.at[mate_rows, 0:1024], val_mate, 2),
+        swap(pull.at[mate_rows, :], pull_mate, 3),
+        swap(colmask.at[mate_rows, :], mask_mate, 4),
+    ]
+    for copy in swaps:
+        copy.start()
     coldec_load.wait()
     coldec[...] = coldec_in[...].astype(BF16)
     rowdec_load.wait()
@@ -258,6 +288,71 @@
                 change = mm(left_side, rhs[unit])
                 out_ref[0, rows, :] = (0.81 * m_ref[rows, :].astype(F32) + FACTOR * change).astype(BF16)
 
+    def by_frequency(first, second):
+        tiles = []
+        for n in range(LOW // 2):
+            one, two = first[8 * n:8 * n + 8], second[8 * n:8 * n + 8]
+            tiles.append(jnp.where(top, one, pltpu.roll(two, 4, 0)))
+            tiles.append(jnp.where(top, pltpu.roll(one, 4, 0), two))
+        return tiles
+
+    def picks_of(a, b):
+        def mixed(ref, cols=slice(0, 128)):
+            rows_a = pl.ds(pl.multiple_of(a * 8, 8), 8)
+            rows_b = pl.ds(pl.multiple_of(b * 8, 8), 8)
+            return jnp.where(top, ref[rows_a, cols], ref[rows_b, cols])
+
+        return mixed(colmask), mixed(pull), [mixed(val, slice(k * 128, (k + 1) * 128)) for k in range(BAND)]
+
+    def pack(stage, tiles, picks):
+        mask, ahead, vals = picks
+        thin = []
+        for k in range(BAND):
+            got = tiles[k]
+            for f in range(k + 1, k + 9):
+                got = jnp.where(vals[k] == f, tiles[f], got)
+            moved = got
+            for shift in range(1, 9):
+                moved = jnp.where(ahead == shift, pltpu.roll(got, 128 - shift, 1), moved)
+            thin.append(moved)
+        for k in range(BAND // 2):
+            packed = jnp.where(lane, thin[k], pltpu.roll(thin[k + BAND // 2], BAND, 1))
+            send[stage, pl.ds(k, 8, stride=4), :] = packed
+
+    def keep(unit, tiles, picks):
+        mask, ahead, vals = picks
+        for f in range(LOW):
+            hit = jnp.zeros((8, 128), F32)
+            for k in range(max(0, f - 8), min(7, f) + 1):
+                hit = jnp.where(vals[k] == f, mask, hit)
+            kept[unit, 8 * f:8 * f + 8, :] = hit * tiles[f]
+
+    def own_base(owner, half):
+        start = pl.multiple_of((owner % 2) * 128 + half * 64, 64)
+        return gm[owner // 2, pl.ds(start, 64), :]
+
+    def ship(stage, owner, i, column):
+        return pltpu.make_async_remote_copy(
+            src_ref=send.at[stage, pl.ds(i * 8, 8), :],
+            dst_ref=recv.at[dp],
+            send_sem=sum_send,
+            recv_sem=sum_recv,
+            device_id=(owner * Y + i, column),
+            device_id_type=MESH,
+        )
+
+    def ship_own(stage, a, b):
+        for i in range(Y):
+            owner = a if i < Y // 2 else b
+
+            @pl.when(owner * Y + i != dp)
+            def _():
+                ship(stage, owner, i, tensor).start()
+
+            @pl.when(owner * Y + i == dp)
+            def _():
+                recv[dp] = send[stage, i * 8:(i + 1) * 8, :]
+
     def pair_step(s, carry):
         owners = owners_of(s)
 
@@ -284,89 +379,66 @@
 
         quarters = [(a, 0) if half == 0 else (b, 1) for a, b in owners for half in range(2)]
         high, low = encode([xt[half_rows(owner, half), :] for owner, half in quarters])
-        grid = mm(jnp.concatenate([high, low, high], axis=1), wx[...])
+        grid = mm(jnp.concatenate([high, low, high], axis=1), wx[:, 0:256])
         grid_a, grid_b = [], []
         for n, (owner, half) in enumerate(quarters):
-            start = pl.multiple_of((owner % 2) * 128 + half * 64, 64)
-            base = gm[owner // 2, pl.ds(start, 64), :]
+            base = own_base(owner, half)
             grid_a.append(grid[n * 64:(n + 1) * 64, :128] + 0.81 * base)
             grid_b.append(grid[n * 64:(n + 1) * 64, 128:] + 0.9 * base)
-
-        def by_frequency(first, second):
-            tiles = []
-            for n in range(LOW // 2):
-                one, two = first[8 * n:8 * n + 8], second[8 * n:8 * n + 8]
-                tiles.append(jnp.where(top, one, pltpu.roll(two, 4, 0)))
-                tiles.append(jnp.where(top, pltpu.roll(one, 4, 0), two))
-            return tiles
-
         for unit, (a, b) in enumerate(owners):
-            def mixed(ref, cols=slice(None)):
-                return jnp.where(top, eight_of(ref, a)[:, cols], eight_of(ref, b)[:, cols])
-
-            mask = mixed(colmask)
-            ahead = mixed(pull)
-            vals = [
-                jnp.where(
-                    top,
-                    val[pl.ds(pl.multiple_of(a * 8, 8), 8), k * 128:(k + 1) * 128],
-                    val[pl.ds(pl.multiple_of(b * 8, 8), 8), k * 128:(k + 1) * 128],
-                )
-                for k in range(BAND)
-            ]
-            for_a = by_frequency(grid_a[2 * unit], grid_a[2 * unit + 1])
-            for_b = by_frequency(grid_b[2 * unit], grid_b[2 * unit + 1])
-            thin = []
-            for k in range(BAND):
-                got = for_b[k]
-                for f in range(k + 1, k + 9):
-                    got = jnp.where(vals[k] == f, for_b[f], got)
-                moved = got
-                for shift in range(1, 9):
-                    moved = jnp.where(ahead == shift, pltpu.roll(got, 128 - shift, 1), moved)
-                thin.append(moved)
-            for k in range(BAND // 2):
-                packed = jnp.where(lane, thin[k], pltpu.roll(thin[k + BAND // 2], BAND, 1))
-                stage = s * 2 + unit
-                send[stage, pl.ds(k, 8, stride=4), :] = packed
-            for f in range(LOW):
-                hit = jnp.zeros((8, 128), F32)
-                for k in range(max(0, f - 8), min(7, f) + 1):
-                    hit = jnp.where(vals[k] == f, mask, hit)
-                kept[s * 2 + unit, 8 * f:8 * f + 8, :] = hit * for_a[f]
-
+            picks = picks_of(a, b)
+            pack(s * 2 + unit, by_frequency(grid_b[2 * unit], grid_b[2 * unit + 1]), picks)
+            keep(s * 2 + unit, by_frequency(grid_a[2 * unit], grid_a[2 * unit + 1]), picks)
         for unit, (a, b) in enumerate(owners):
-            for i in range(Y):
-                owner = a if i < Y // 2 else b
-                tile = send.at[s * 2 + unit, pl.ds(i * 8, 8), :]
-
-                @pl.when(owner * Y + i != dp)
-                def _():
-                    pltpu.make_async_remote_copy(
-                        src_ref=tile,
-                        dst_ref=recv.at[dp],
-                        send_sem=sum_send,
-                        recv_sem=sum_recv,
-                        device_id=(owner * Y + i, tensor),
-                        device_id_type=MESH,
-                    ).start()
-
-                @pl.when(owner * Y + i == dp)
-                def _():
-                    recv[dp] = send[s * 2 + unit, i * 8:(i + 1) * 8, :]
-
+            ship_own(s * 2 + unit, a, b)
         return carry
 
-    lax.fori_loop(0, X, pair_step, 0)
+    lax.fori_loop(0, X - 1, pair_step, 0)
+
+    for copy in swaps:
+        copy.wait_recv()
+    for half in range(2):
+        half_copy(far, half, mate).wait_recv()
+        half_copy(far, half, mate).start()
+    high, low = encode([xt[half_rows(far, half), :] for half in range(2)])
+    grid = mm(jnp.concatenate([high, low, high], axis=1), wx[...])
+    bases = [own_base(far, half) for half in range(2)]
+    picks = picks_of(far, far)
+    pack(6, by_frequency(*[grid[n * 64:(n + 1) * 64, 128:256] + 0.9 * bases[n] for n in range(2)]), picks)
+    ship_own(6, far, far)
+    theirs = (mask_mate[...], pull_mate[...], [val_mate[:, k * 128:(k + 1) * 128] for k in range(BAND)])
+    pack(8, by_frequency(*[grid[n * 64:(n + 1) * 64, 256:] + 0.9 * gm_mate[n * 64:(n + 1) * 64, :] for n in range(2)]), theirs)
+    for i in range(Y):
+        ship(8, far, i, mate).start()
+    keep(6, by_frequency(*[grid[n * 64:(n + 1) * 64, :128] + 0.81 * bases[n] for n in range(2)]), picks)
+
+    write_pair(X - 2)
+    for half in range(2):
+        half_copy(far_mate, half, mate).wait_recv()
+    high, low = encode([xt[half_rows(far_mate, half), :] for half in range(2)])
+    grid = mm(jnp.concatenate([high, low, high], axis=1), wx[:, 0:128])
+    picks = picks_of(far_mate, far_mate)
+    keep(7, by_frequency(*[grid[n * 64:(n + 1) * 64] + 0.81 * own_base(far_mate, n) for n in range(2)]), picks)
     write_pair(X - 1)
 
     for k in range(BAND):
         own[k] = val[pl.ds(pl.multiple_of(cz * 8, 8), 8), k * 128:(k + 1) * 128]
     own[BAND] = eight_of(push, cz)
-    everyone = recv.at[pl.ds(0, GROUPS - 1)]
-    pltpu.make_async_copy(everyone, everyone, sum_recv).wait()
-    everyone_sent = recv.at[pl.ds(0, GROUPS - 1)]
-    pltpu.make_async_copy(everyone_sent, everyone_sent, sum_send).wait()
+    def wait_sums(count):
+        some = recv.at[pl.ds(0, count)]
+        pltpu.make_async_copy(some, some, sum_recv).wait()
+        pltpu.make_async_copy(some, some, sum_send).wait()
+
+    @pl.when(crossed)
+    def _():
+        wait_sums(GROUPS)
+
+    @pl.when(jnp.logical_not(crossed))
+    def _():
+        wait_sums(GROUPS - 1)
+
+    for copy in swaps:
+        copy.wait_send()
     sent = xt.at[pl.ds(0, 7 * SHARD), :]
     pltpu.make_async_copy(sent, sent, gather_send).wait()
 
@@ -449,17 +521,23 @@
             pltpu.VMEM((64, 128), F32),
             pltpu.VMEM((64, 128), F32),
             pltpu.VMEM((64, 128), F32),
-            pltpu.VMEM((768, 256), BF16),
+            pltpu.VMEM((768, 384), BF16),
             pltpu.VMEM((2, 768, COLS), BF16),
             pltpu.VMEM((X, 256, 128), F32),
             pltpu.VMEM((CHUNKS, 128, 128), F32),
-            pltpu.VMEM((CHUNKS, 32, 128), F32),
+            pltpu.VMEM((CHUNKS + 1, 32, 128), F32),
+            pltpu.VMEM((128, 128), F32),
+            pltpu.VMEM((8, 1024), F32),
+            pltpu.VMEM((8, 128), F32),
+            pltpu.VMEM((8, 128), F32),
             pltpu.SemaphoreType.DMA((8,)),
             pltpu.SemaphoreType.DMA((X,)),
             pltpu.SemaphoreType.DMA,
             pltpu.SemaphoreType.DMA((CHUNKS * 2,)),
             pltpu.SemaphoreType.DMA,
             pltpu.SemaphoreType.DMA,
+            pltpu.SemaphoreType.DMA((5,)),
+            pltpu.SemaphoreType.DMA((5,)),
         ],
         compiler_params=pltpu.CompilerParams(
             collective_id=0, has_side_effects=True, vmem_limit_bytes=40 * 1024 * 1024

time: 30.9 us -> 30.2 us (0.977); the launches traced: 30.9 us -> 29.8 us
  Pallas kernels: 30.2 us -> 29.2 us
    pallas_call x1, Pallas kernels: 27.8 us -> 26.7 us  [shards(): pl.pallas_call(kernel, out_shape=(pltpu.VMEM(momentum.shape, BF16), pltpu...]
where the time goes in v4:
time: 30.2 us; the launch traced here: 29.8 us
  Pallas kernels  29.2 us (97%)
  between operations  0.64 us (2%)
    pallas_call x1, Pallas kernels, shards(): pl.pallas_call(kernel, out_shape=(pltpu.VMEM(momentum.shape, BF16), pltpu...  26.7 us
    pallas_call x1, Pallas kernels, shards(): pl.pallas_call(finish, out_shape=(pltpu.HBM(momentum.shape, BF16), pltpu....  2.46 us

profile of v4, /device:TPU:5, one launch (start us, length us, event | category | flops | bytes accessed | tf_op | source)
XLA Modules:
  0.0 29.8 jit_solution(16601979684134840684)
XLA Ops:
  0.6 26.7 %demo_steps.1 = (bf16[1,4096,512]{2,1,0:T(8,128)(2,1)S(1)}, f32[32,8,128]{2,1,0:T(8,128)S(1)}, f32[9,8,128]{2,1,0:T(8,128)S(1)}, bf16[256,512]{1,0:T(8,128)(2,1)S(1)}, bf16[512,256]{1,0:T(8,128)(2,1)S(1)}) custom-call(bf16[2,128,512]{2,1,0:T(8,128)(2,1)} %x_hbm.1, bf16[2,128,512]{2,1,0:T(8,128)(2,1)} %d_hbm.1, bf16[1,4096,512]{2,1,0:T(8,128)(2,1)} %m_hbm.1, ...), custom_call_target="tpu_custom_call" | custom-call | tf_op jit(solution)/shard_map/demo_steps/pallas_call | solution.py:497
  27.3 2.5 %demo_finish.1 = (bf16[1,4096,512]{2,1,0:T(8,128)(2,1)}, f32[128,512]{1,0:T(8,128)}) custom-call(bf16[1,4096,512]{2,1,0:T(8,128)(2,1)S(1)} %get-tuple-element.7.new_ref, f32[32,8,128]{2,1,0:T(8,128)S(1)} %get-tuple-element.8.recv, f32[9,8,128]{2,1,0:T(8,128)S(1)} %get-tuple-element.9.own, bf16[256,512]{1,0:T(8,128)(2,1)S(1)} %get-tuple-element.10.coldec, ...), custom_call_target="tpu_custom_call" | custom-call | tf_op jit(solution)/shard_map/demo_finish/pallas_call | solution.py:548

commit v5 on v4

--- a/solution.py
+++ b/solution.py
@@ -24,9 +24,10 @@
 X = 4
 GROUPS = 32
 Y = 4
+Z = 8
 HALF = SHARD // 2
 CHUNKS = 8
-PARTS = 8
+PARTS = 1
 FACTOR = 1.0 / math.sqrt(TOK)
 
 
@@ -89,6 +90,7 @@
     xin, din, m_ref, band_ref, rowenc_in, rowdec_in, colenc_in, coldec_in, rowenc, colenc,
     xt, val, colmask, pull, push, wx, rhs, gm, kept, send, gm_mate, val_mate, pull_mate, mask_mate,
     load_sem, m_sem, gather_send, gather_recv, sum_send, sum_recv, swap_send, swap_recv,
+    z_token, y_token, mate_token,
 ):
     dp = lax.axis_index("dp")
     tensor = lax.axis_index("tensor")
@@ -116,9 +118,16 @@
         load(x_hbm.at[:, :, half * 256:(half + 1) * 256], xin.at[:, :, half * 256:(half + 1) * 256], half)
         for half in range(2)
     ]
+    def column(dz, dy):
+        return (cz + dz) % Z * Y + (cy + dy) % Y
+
+    z_far = [column(2, 0), column(Z - 2, 0)]
+    y_peers = [column(0, n) for n in range(1, Y)]
+    near = [(dp, mate), (dp, right), (dp, left)]
+    near += [(peer, tensor) for peer in (column(1, 0), column(Z - 1, 0), *z_far, *y_peers)]
     barrier = pltpu.get_barrier_semaphore()
-    for peer in (mate, right, left):
-        pl.semaphore_signal(barrier, inc=1, device_id=(dp, peer), device_id_type=MESH)
+    for peer in near:
+        pl.semaphore_signal(barrier, inc=1, device_id=peer, device_id_type=MESH)
     colenc_load = load(colenc_hbm, colenc_in, 2)
     d_load = load(d_hbm, din, 3)
     band_load = load(band_hbm, band_ref, 4)
@@ -132,24 +141,6 @@
 
     for p in range(X):
         m_copy(p).start()
-
-    def greet(i, carry):
-        pl.semaphore_signal(
-            barrier, inc=1, device_id=((dp + i) % GROUPS, tensor), device_id_type=MESH
-        )
-        return carry
-
-    lax.fori_loop(1, GROUPS, greet, 0)
-
-    @pl.when(crossed)
-    def _():
-        def greet_mates(i, carry):
-            pl.semaphore_signal(
-                barrier, inc=1, device_id=((dp + i) % GROUPS, mate), device_id_type=MESH
-            )
-            return carry
-
-        lax.fori_loop(1, GROUPS, greet_mates, 0)
 
     def half_copy(owner, half, target):
         rows = pl.ds(pl.multiple_of(owner * SHARD + half * HALF, HALF), HALF)
@@ -169,7 +160,7 @@
             xt[rows, step * TOK:(step + 1) * TOK] = xin[step, :, half * HALF:(half + 1) * HALF].T
 
     turn(0)
-    pl.semaphore_wait(barrier, 3 + GROUPS - 1 + jnp.where(cz == far, Y - 1, Y))
+    pl.semaphore_wait(barrier, len(near))
     half_copy(tensor, 0, right).start()
     turn(1)
     half_copy(tensor, 1, left).start()
@@ -177,6 +168,9 @@
     half_copy(tensor, 1, mate).start()
     half_copy(tensor, 1, right).start()
     half_copy(tensor, 0, left).start()
+
+    for peer in z_far:
+        pl.semaphore_signal(z_token, inc=1, device_id=(peer, tensor), device_id_type=MESH)
 
     colenc_load.wait()
     colenc[...] = colenc_in[...].astype(BF16)
@@ -233,7 +227,14 @@
         gm[p] = both[:256, :128] + both[:256, 128:] + both[256:, :128]
         return carry
 
+    pl.semaphore_wait(z_token, 2)
+    for peer in y_peers:
+        pl.semaphore_signal(y_token, inc=1, device_id=(peer, tensor), device_id_type=MESH)
+
     lax.fori_loop(0, X, momentum_step, 0)
+
+    pl.semaphore_wait(y_token, Y - 1)
+    pl.semaphore_signal(mate_token, inc=1, device_id=(dp, mate), device_id_type=MESH)
 
     def swap(src, dst, n):
         return pltpu.make_async_remote_copy(
@@ -395,6 +396,7 @@
 
     lax.fori_loop(0, X - 1, pair_step, 0)
 
+    pl.semaphore_wait(mate_token, 1)
     for copy in swaps:
         copy.wait_recv()
     for half in range(2):
@@ -538,6 +540,9 @@
             pltpu.SemaphoreType.DMA,
             pltpu.SemaphoreType.DMA((5,)),
             pltpu.SemaphoreType.DMA((5,)),
+            pltpu.SemaphoreType.REGULAR,
+            pltpu.SemaphoreType.REGULAR,
+            pltpu.SemaphoreType.REGULAR,
         ],
         compiler_params=pltpu.CompilerParams(
             collective_id=0, has_side_effects=True, vmem_limit_bytes=40 * 1024 * 1024

time: 30.2 us -> 28.1 us (0.930)
  Pallas kernels: 29.2 us -> 27.3 us
    pallas_call x1, Pallas kernels: 26.7 us -> 25.1 us  [shards(): pl.pallas_call(kernel, out_shape=(pltpu.VMEM(momentum.shape, BF16), pltpu...]
where the time goes in v5:
time: 28.1 us; the launch traced here: 28 us
  Pallas kernels  27.3 us (97%)
  between operations  0.64 us (2%)
    pallas_call x1, Pallas kernels, shards(): pl.pallas_call(kernel, out_shape=(pltpu.VMEM(momentum.shape, BF16), pltpu...  25.1 us
    pallas_call x1, Pallas kernels, shards(): pl.pallas_call(finish, out_shape=(pltpu.HBM(momentum.shape, BF16), pltpu....  2.23 us

profile of v5, /device:TPU:5, one launch (start us, length us, event | category | flops | bytes accessed | tf_op | source)
XLA Modules:
  0.0 28.0 jit_solution(5996268547169782593)
XLA Ops:
  0.6 25.1 %demo_steps.1 = (bf16[1,4096,512]{2,1,0:T(8,128)(2,1)S(1)}, f32[32,8,128]{2,1,0:T(8,128)S(1)}, f32[9,8,128]{2,1,0:T(8,128)S(1)}, bf16[256,512]{1,0:T(8,128)(2,1)S(1)}, bf16[512,256]{1,0:T(8,128)(2,1)S(1)}) custom-call(bf16[2,128,512]{2,1,0:T(8,128)(2,1)} %x_hbm.1, bf16[2,128,512]{2,1,0:T(8,128)(2,1)} %d_hbm.1, bf16[1,4096,512]{2,1,0:T(8,128)(2,1)} %m_hbm.1, ...), custom_call_target="tpu_custom_call" | custom-call | tf_op jit(solution)/shard_map/demo_steps/pallas_call | solution.py:499
  25.8 2.2 %demo_finish.1 = (bf16[1,4096,512]{2,1,0:T(8,128)(2,1)}, f32[128,512]{1,0:T(8,128)}) custom-call(bf16[1,4096,512]{2,1,0:T(8,128)(2,1)S(1)} %get-tuple-element.7.new_ref, f32[32,8,128]{2,1,0:T(8,128)S(1)} %get-tuple-element.8.recv, f32[9,8,128]{2,1,0:T(8,128)S(1)} %get-tuple-element.9.own, bf16[256,512]{1,0:T(8,128)(2,1)S(1)} %get-tuple-element.10.coldec, ...), custom_call_target="tpu_custom_call" | custom-call | tf_op jit(solution)/shard_map/demo_finish/pallas_call | solution.py:553

commit v6 on v5

--- a/solution.py
+++ b/solution.py
@@ -227,14 +227,11 @@
         gm[p] = both[:256, :128] + both[:256, 128:] + both[256:, :128]
         return carry
 
+    lax.fori_loop(0, X, momentum_step, 0)
+
     pl.semaphore_wait(z_token, 2)
     for peer in y_peers:
         pl.semaphore_signal(y_token, inc=1, device_id=(peer, tensor), device_id_type=MESH)
-
-    lax.fori_loop(0, X, momentum_step, 0)
-
-    pl.semaphore_wait(y_token, Y - 1)
-    pl.semaphore_signal(mate_token, inc=1, device_id=(dp, mate), device_id_type=MESH)
 
     def swap(src, dst, n):
         return pltpu.make_async_remote_copy(
@@ -372,6 +369,10 @@
             @pl.when(s == 1)
             def _():
                 half_copy(right, 1, left).start()
+                pl.semaphore_wait(y_token, Y - 1)
+                pl.semaphore_signal(mate_token, inc=1, device_id=(dp, mate), device_id_type=MESH)
+                for unit, (a, b) in enumerate(owners_of(0)):
+                    ship_own(unit, a, b)
 
             write_pair(s - 1)
 
@@ -390,8 +391,12 @@
             picks = picks_of(a, b)
             pack(s * 2 + unit, by_frequency(grid_b[2 * unit], grid_b[2 * unit + 1]), picks)
             keep(s * 2 + unit, by_frequency(grid_a[2 * unit], grid_a[2 * unit + 1]), picks)
-        for unit, (a, b) in enumerate(owners):
-            ship_own(s * 2 + unit, a, b)
+
+        @pl.when(s > 0)
+        def _():
+            for unit, (a, b) in enumerate(owners):
+                ship_own(s * 2 + unit, a, b)
+
         return carry
 
     lax.fori_loop(0, X - 1, pair_step, 0)
@@ -403,16 +408,18 @@
         half_copy(far, half, mate).wait_recv()
         half_copy(far, half, mate).start()
     high, low = encode([xt[half_rows(far, half), :] for half in range(2)])
-    grid = mm(jnp.concatenate([high, low, high], axis=1), wx[...])
+    triple = jnp.concatenate([high, low, high], axis=1)
+    grid = mm(triple, wx[:, 128:384])
     bases = [own_base(far, half) for half in range(2)]
     picks = picks_of(far, far)
-    pack(6, by_frequency(*[grid[n * 64:(n + 1) * 64, 128:256] + 0.9 * bases[n] for n in range(2)]), picks)
+    pack(6, by_frequency(*[grid[n * 64:(n + 1) * 64, :128] + 0.9 * bases[n] for n in range(2)]), picks)
     ship_own(6, far, far)
     theirs = (mask_mate[...], pull_mate[...], [val_mate[:, k * 128:(k + 1) * 128] for k in range(BAND)])
-    pack(8, by_frequency(*[grid[n * 64:(n + 1) * 64, 256:] + 0.9 * gm_mate[n * 64:(n + 1) * 64, :] for n in range(2)]), theirs)
+    pack(8, by_frequency(*[grid[n * 64:(n + 1) * 64, 128:] + 0.9 * gm_mate[n * 64:(n + 1) * 64, :] for n in range(2)]), theirs)
     for i in range(Y):
         ship(8, far, i, mate).start()
-    keep(6, by_frequency(*[grid[n * 64:(n + 1) * 64, :128] + 0.81 * bases[n] for n in range(2)]), picks)
+    grid = mm(triple, wx[:, 0:128])
+    keep(6, by_frequency(*[grid[n * 64:(n + 1) * 64] + 0.81 * bases[n] for n in range(2)]), picks)
 
     write_pair(X - 2)
     for half in range(2):

time: 28.1 us -> 27.6 us (0.982)
  Pallas kernels: 27.3 us -> 26.9 us
    pallas_call x1, Pallas kernels: 25.1 us -> 24.7 us  [shards(): pl.pallas_call(kernel, out_shape=(pltpu.VMEM(momentum.shape, BF16), pltpu...]
where the time goes in v6:
time: 27.6 us; the launch traced here: 27.5 us
  Pallas kernels  26.9 us (97%)
  between operations  0.64 us (2%)
    pallas_call x1, Pallas kernels, shards(): pl.pallas_call(kernel, out_shape=(pltpu.VMEM(momentum.shape, BF16), pltpu...  24.7 us
    pallas_call x1, Pallas kernels, shards(): pl.pallas_call(finish, out_shape=(pltpu.HBM(momentum.shape, BF16), pltpu....  2.23 us

profile of v6, /device:TPU:5, one launch (start us, length us, event | category | flops | bytes accessed | tf_op | source)
XLA Modules:
  0.0 27.5 jit_solution(14132827659712663004)
XLA Ops:
  0.6 24.7 %demo_steps.1 = (bf16[1,4096,512]{2,1,0:T(8,128)(2,1)S(1)}, f32[32,8,128]{2,1,0:T(8,128)S(1)}, f32[9,8,128]{2,1,0:T(8,128)S(1)}, bf16[256,512]{1,0:T(8,128)(2,1)S(1)}, bf16[512,256]{1,0:T(8,128)(2,1)S(1)}) custom-call(bf16[2,128,512]{2,1,0:T(8,128)(2,1)} %x_hbm.1, bf16[2,128,512]{2,1,0:T(8,128)(2,1)} %d_hbm.1, bf16[1,4096,512]{2,1,0:T(8,128)(2,1)} %m_hbm.1, ...), custom_call_target="tpu_custom_call" | custom-call | tf_op jit(solution)/shard_map/demo_steps/pallas_call | solution.py:506
  25.3 2.2 %demo_finish.1 = (bf16[1,4096,512]{2,1,0:T(8,128)(2,1)}, f32[128,512]{1,0:T(8,128)}) custom-call(bf16[1,4096,512]{2,1,0:T(8,128)(2,1)S(1)} %get-tuple-element.7.new_ref, f32[32,8,128]{2,1,0:T(8,128)S(1)} %get-tuple-element.8.recv, f32[9,8,128]{2,1,0:T(8,128)S(1)} %get-tuple-element.9.own, bf16[256,512]{1,0:T(8,128)(2,1)S(1)} %get-tuple-element.10.coldec, ...), custom_call_target="tpu_custom_call" | custom-call | tf_op jit(solution)/shard_map/demo_finish/pallas_call | solution.py:560

commit v7 on v6

--- a/solution.py
+++ b/solution.py
@@ -90,7 +90,7 @@
     xin, din, m_ref, band_ref, rowenc_in, rowdec_in, colenc_in, coldec_in, rowenc, colenc,
     xt, val, colmask, pull, push, wx, rhs, gm, kept, send, gm_mate, val_mate, pull_mate, mask_mate,
     load_sem, m_sem, gather_send, gather_recv, sum_send, sum_recv, swap_send, swap_recv,
-    z_token, y_token, mate_token,
+    near_token, z_token, y_token, mate_token,
 ):
     dp = lax.axis_index("dp")
     tensor = lax.axis_index("tensor")
@@ -124,7 +124,8 @@
     z_far = [column(2, 0), column(Z - 2, 0)]
     y_peers = [column(0, n) for n in range(1, Y)]
     near = [(dp, mate), (dp, right), (dp, left)]
-    near += [(peer, tensor) for peer in (column(1, 0), column(Z - 1, 0), *z_far, *y_peers)]
+    beside = [column(1, 0), column(Z - 1, 0), column(0, 1), column(0, Y - 1)]
+    near += [(peer, tensor) for peer in beside]
     barrier = pltpu.get_barrier_semaphore()
     for peer in near:
         pl.semaphore_signal(barrier, inc=1, device_id=peer, device_id_type=MESH)
@@ -160,17 +161,17 @@
             xt[rows, step * TOK:(step + 1) * TOK] = xin[step, :, half * HALF:(half + 1) * HALF].T
 
     turn(0)
+    turn(1)
     pl.semaphore_wait(barrier, len(near))
     half_copy(tensor, 0, right).start()
-    turn(1)
     half_copy(tensor, 1, left).start()
+    half_copy(tensor, 1, right).start()
+    half_copy(tensor, 0, left).start()
     half_copy(tensor, 0, mate).start()
     half_copy(tensor, 1, mate).start()
-    half_copy(tensor, 1, right).start()
-    half_copy(tensor, 0, left).start()
-
-    for peer in z_far:
-        pl.semaphore_signal(z_token, inc=1, device_id=(peer, tensor), device_id_type=MESH)
+
+    for peer in beside:
+        pl.semaphore_signal(near_token, inc=1, device_id=(peer, tensor), device_id_type=MESH)
 
     colenc_load.wait()
     colenc[...] = colenc_in[...].astype(BF16)
@@ -208,6 +209,10 @@
     colmask[...] = seen
     pull[...] = ahead
     push[...] = back
+
+    pl.semaphore_wait(near_token, len(beside))
+    for peer in z_far:
+        pl.semaphore_signal(z_token, inc=1, device_id=(peer, tensor), device_id_type=MESH)
 
     rowenc_load.wait()
     rowenc[...] = rowenc_in[...].astype(BF16)
@@ -550,6 +555,7 @@
             pltpu.SemaphoreType.REGULAR,
             pltpu.SemaphoreType.REGULAR,
             pltpu.SemaphoreType.REGULAR,
+            pltpu.SemaphoreType.REGULAR,
         ],
         compiler_params=pltpu.CompilerParams(
             collective_id=0, has_side_effects=True, vmem_limit_bytes=40 * 1024 * 1024

time: 27.6 us -> 27.4 us (level)
  no operation moved by 1% of the time
where the time goes in v7:
time: 27.4 us
  Pallas kernels  26.7 us (97%)
  between operations  0.64 us (2%)
    pallas_call x1, Pallas kernels, shards(): pl.pallas_call(kernel, out_shape=(pltpu.VMEM(momentum.shape, BF16), pltpu...  24.5 us
    pallas_call x1, Pallas kernels, shards(): pl.pallas_call(finish, out_shape=(pltpu.HBM(momentum.shape, BF16), pltpu....  2.23 us

profile of v7, /device:TPU:5, one launch (start us, length us, event | category | flops | bytes accessed | tf_op | source)
XLA Modules:
  0.0 27.4 jit_solution(13425238763667500027)
XLA Ops:
  0.6 24.5 %demo_steps.1 = (bf16[1,4096,512]{2,1,0:T(8,128)(2,1)S(1)}, f32[32,8,128]{2,1,0:T(8,128)S(1)}, f32[9,8,128]{2,1,0:T(8,128)S(1)}, bf16[256,512]{1,0:T(8,128)(2,1)S(1)}, bf16[512,256]{1,0:T(8,128)(2,1)S(1)}) custom-call(bf16[2,128,512]{2,1,0:T(8,128)(2,1)} %x_hbm.1, bf16[2,128,512]{2,1,0:T(8,128)(2,1)} %d_hbm.1, bf16[1,4096,512]{2,1,0:T(8,128)(2,1)} %m_hbm.1, ...), custom_call_target="tpu_custom_call" | custom-call | tf_op jit(solution)/shard_map/demo_steps/pallas_call | solution.py:511
  25.1 2.2 %demo_finish.1 = (bf16[1,4096,512]{2,1,0:T(8,128)(2,1)}, f32[128,512]{1,0:T(8,128)}) custom-call(bf16[1,4096,512]{2,1,0:T(8,128)(2,1)S(1)} %get-tuple-element.7.new_ref, f32[32,8,128]{2,1,0:T(8,128)S(1)} %get-tuple-element.8.recv, f32[9,8,128]{2,1,0:T(8,128)S(1)} %get-tuple-element.9.own, bf16[256,512]{1,0:T(8,128)(2,1)S(1)} %get-tuple-element.10.coldec, ...), custom_call_target="tpu_custom_call" | custom-call | tf_op jit(solution)/shard_map/demo_finish/pallas_call | solution.py:566

commit v8 on v7

--- a/solution.py
+++ b/solution.py
@@ -362,18 +362,22 @@
         @pl.when(s > 0)
         def _():
             half_copy(owners[0][0], 0, mate).wait_recv()
-            half_copy(owners[0][0], 0, mate).start()
 
             @pl.when(s == 1)
             def _():
                 half_copy(left, 0, right).start()
 
+            half_copy(owners[0][0], 0, mate).start()
             half_copy(owners[0][1], 1, mate).wait_recv()
-            half_copy(owners[0][1], 1, mate).start()
 
             @pl.when(s == 1)
             def _():
                 half_copy(right, 1, left).start()
+
+            half_copy(owners[0][1], 1, mate).start()
+
+            @pl.when(s == 1)
+            def _():
                 pl.semaphore_wait(y_token, Y - 1)
                 pl.semaphore_signal(mate_token, inc=1, device_id=(dp, mate), device_id_type=MESH)
                 for unit, (a, b) in enumerate(owners_of(0)):
@@ -411,7 +415,6 @@
         copy.wait_recv()
     for half in range(2):
         half_copy(far, half, mate).wait_recv()
-        half_copy(far, half, mate).start()
     high, low = encode([xt[half_rows(far, half), :] for half in range(2)])
     triple = jnp.concatenate([high, low, high], axis=1)
     grid = mm(triple, wx[:, 128:384])
@@ -423,6 +426,8 @@
     pack(8, by_frequency(*[grid[n * 64:(n + 1) * 64, 128:] + 0.9 * gm_mate[n * 64:(n + 1) * 64, :] for n in range(2)]), theirs)
     for i in range(Y):
         ship(8, far, i, mate).start()
+    for half in range(2):
+        half_copy(far, half, mate).start()
     grid = mm(triple, wx[:, 0:128])
     keep(6, by_frequency(*[grid[n * 64:(n + 1) * 64] + 0.81 * bases[n] for n in range(2)]), picks)
 

time: 27.4 us -> 27.4 us (level)
  no operation moved by 1% of the time
where the time goes in v8:
time: 27.4 us
  Pallas kernels  26.7 us (97%)
  between operations  0.64 us (2%)
    pallas_call x1, Pallas kernels, shards(): pl.pallas_call(kernel, out_shape=(pltpu.VMEM(momentum.shape, BF16), pltpu...  24.5 us
    pallas_call x1, Pallas kernels, shards(): pl.pallas_call(finish, out_shape=(pltpu.HBM(momentum.shape, BF16), pltpu....  2.23 us

profile of v8, /device:TPU:5, one launch (start us, length us, event | category | flops | bytes accessed | tf_op | source)
XLA Modules:
  0.0 27.4 jit_solution(9620778887919765048)
XLA Ops:
  0.6 24.5 %demo_steps.1 = (bf16[1,4096,512]{2,1,0:T(8,128)(2,1)S(1)}, f32[32,8,128]{2,1,0:T(8,128)S(1)}, f32[9,8,128]{2,1,0:T(8,128)S(1)}, bf16[256,512]{1,0:T(8,128)(2,1)S(1)}, bf16[512,256]{1,0:T(8,128)(2,1)S(1)}) custom-call(bf16[2,128,512]{2,1,0:T(8,128)(2,1)} %x_hbm.1, bf16[2,128,512]{2,1,0:T(8,128)(2,1)} %d_hbm.1, bf16[1,4096,512]{2,1,0:T(8,128)(2,1)} %m_hbm.1, ...), custom_call_target="tpu_custom_call" | custom-call | tf_op jit(solution)/shard_map/demo_steps/pallas_call | solution.py:516
  25.1 2.2 %demo_finish.1 = (bf16[1,4096,512]{2,1,0:T(8,128)(2,1)}, f32[128,512]{1,0:T(8,128)}) custom-call(bf16[1,4096,512]{2,1,0:T(8,128)(2,1)S(1)} %get-tuple-element.7.new_ref, f32[32,8,128]{2,1,0:T(8,128)S(1)} %get-tuple-element.8.recv, f32[9,8,128]{2,1,0:T(8,128)S(1)} %get-tuple-element.9.own, bf16[256,512]{1,0:T(8,128)(2,1)S(1)} %get-tuple-element.10.coldec, ...), custom_call_target="tpu_custom_call" | custom-call | tf_op jit(solution)/shard_map/demo_finish/pallas_call | solution.py:571
